TPU v7x, 128 devices: a whole 4x4x4 slice. The times are simulated.
128 devices in a mesh: fsdp: 16 (over x_hi, z, core), tensor: 8 (over x_lo, y).
Axes of the slice: x: 4 (x_hi: 2, x_lo: 2; x = x_hi * 2 + x_lo), y: 4, z: 4, core: 2. Of those that a mesh axis runs over, the one named last changes fastest.
Arguments:
- tokens: bfloat16 [8192, 4096], P('fsdp'), may hold values from -48 to 48
- token_ids: int32 [8192], P('fsdp'), may hold values from 0 to 128000, as said below
- out_grad: bfloat16 [8192, 4096], P('fsdp', 'tensor'), may hold values from -0.5 to 0.5
- w_query: bfloat16 [4096, 4096], P('fsdp', 'tensor'), may hold values from -0.09375 to 0.09375
- w_key: bfloat16 [4096, 1024], P('fsdp', 'tensor'), may hold values from -0.09375 to 0.09375
- w_value: bfloat16 [4096, 1024], P('fsdp', 'tensor'), may hold values from -0.09375 to 0.09375
- dec_states: bfloat16 [128, 2, 4096], P('fsdp'), may hold values from -48 to 48
- cache_lens: int32 [128], P('fsdp'), may hold values from 1 to 2048, as said below
- key_cache: bfloat16 [128, 2048, 1024], P('fsdp', None, 'tensor'), may hold values from -48 to 48
- value_cache: bfloat16 [128, 2048, 1024], P('fsdp', None, 'tensor'), may hold values from -6 to 6
Outputs:
- grad_query: bfloat16 [4096, 4096], P('fsdp', 'tensor')
- grad_key: bfloat16 [4096, 1024], P('fsdp', 'tensor')
- grad_value: bfloat16 [4096, 1024], P('fsdp', 'tensor')
- input_grad: bfloat16 [8192, 4096], P('fsdp', 'tensor')
- dec_out: bfloat16 [128, 2, 4096], P('fsdp', None, 'tensor')
Inputs may be any that keep to these rules, and one draw needn't show every extreme that they name: `token_ids`: position 0 of every block of 512 tokens holds the begin-of-document id 128000, which marks the first position of each packed document; other ids lie below it. `cache_lens`: positions at or past a row's length hold stale entries.
All inputs are finite; a program needn't handle non-finite values.
Results may differ from a plain program's by a relative error of at most 0.035.
Values may be sent and summed in bfloat16 or wider, within the bound.
A program may use at most 128 MiB of HBM per device.

v0:
```python
import math

import jax
import jax.numpy as jnp
from jax import lax
from jax.sharding import PartitionSpec as P

HD = 128


learn_rate = 0.004
bos_id = 128000


def local_grads(tokens, token_ids, out_grad, gathered, q_cols, kv_cols):
    width = tokens.shape[0]
    kv_heads = kv_cols // HD
    groups = q_cols // kv_cols
    scale = 1.0 / math.sqrt(HD)
    projected = jnp.dot(tokens, gathered, preferred_element_type=jnp.float32).astype(jnp.bfloat16)
    query = projected[:, :q_cols].reshape(width, kv_heads, groups, HD)
    keys = projected[:, q_cols : q_cols + kv_cols].reshape(width, kv_heads, HD)
    values = projected[:, q_cols + kv_cols :].reshape(width, kv_heads, HD)
    segment = jnp.cumsum((token_ids == bos_id).astype(jnp.int32))
    place = jnp.arange(width)
    allowed = (place[:, None] >= place[None, :]) & (segment[:, None] == segment[None, :])
    scores = jnp.einsum("ihgd,jhd->hgij", query, keys, preferred_element_type=jnp.float32) * scale
    scores = jnp.where(allowed, scores, -jnp.inf)
    top = jnp.max(scores, -1, keepdims=True)
    expo = jnp.exp(scores - top)
    probs = expo / jnp.sum(expo, -1, keepdims=True)
    probs_b = probs.astype(jnp.bfloat16)
    upstream = out_grad.reshape(width, kv_heads, groups, HD)
    dprob = jnp.einsum("ihgd,jhd->hgij", upstream, values, preferred_element_type=jnp.float32)
    delta = jnp.sum(probs * dprob, -1, keepdims=True)
    dscore = (probs * (dprob - delta) * scale).astype(jnp.bfloat16)
    grad_q = jnp.einsum("hgij,jhd->ihgd", dscore, keys, preferred_element_type=jnp.float32).astype(
        jnp.bfloat16
    )
    grad_k = jnp.einsum("hgij,ihgd->jhd", dscore, query, preferred_element_type=jnp.float32).astype(
        jnp.bfloat16
    )
    grad_v = jnp.einsum(
        "hgij,ihgd->jhd", probs_b, upstream, preferred_element_type=jnp.float32
    ).astype(jnp.bfloat16)
    return jnp.concatenate(
        [
            grad_q.reshape(width, q_cols),
            grad_k.reshape(width, kv_cols),
            grad_v.reshape(width, kv_cols),
        ],
        1,
    )


def decode_steps(dec_states, cache_lens, key_cache, value_cache, fresh_full, q_cols, kv_cols):
    rows = dec_states.shape[0]
    cache_len = key_cache.shape[1]
    kv_heads = kv_cols // HD
    groups = q_cols // kv_cols
    scale = 1.0 / math.sqrt(HD)
    flat = dec_states.reshape(rows * 2, dec_states.shape[2])
    projected = jnp.dot(flat, fresh_full, preferred_element_type=jnp.float32).astype(jnp.bfloat16)
    dec_q = projected[:, :q_cols].reshape(rows, 2, kv_heads, groups, HD)
    dec_k = projected[:, q_cols : q_cols + kv_cols].reshape(rows, 2, kv_heads, HD)
    dec_v = projected[:, q_cols + kv_cols :].reshape(rows, 2, kv_heads, HD)
    cached_k = key_cache.reshape(rows, cache_len, kv_heads, HD)
    cached_v = value_cache.reshape(rows, cache_len, kv_heads, HD)
    older = (
        jnp.einsum("rshgd,rjhd->rshgj", dec_q, cached_k, preferred_element_type=jnp.float32) * scale
    )
    valid = jnp.arange(cache_len)[None, :] < cache_lens[:, None]
    older = jnp.where(valid[:, None, None, None, :], older, -jnp.inf)
    newer = (
        jnp.einsum("rshgd,rthd->rshgt", dec_q, dec_k, preferred_element_type=jnp.float32) * scale
    )
    causal = jnp.arange(2)[:, None] >= jnp.arange(2)[None, :]
    newer = jnp.where(causal[None, :, None, None, :], newer, -jnp.inf)
    top = jnp.maximum(jnp.max(older, -1, keepdims=True), jnp.max(newer, -1, keepdims=True))
    exp_old = jnp.exp(older - top)
    exp_new = jnp.exp(newer - top)
    denom = jnp.sum(exp_old, -1, keepdims=True) + jnp.sum(exp_new, -1, keepdims=True)
    prob_old = (exp_old / denom).astype(jnp.bfloat16)
    prob_new = (exp_new / denom).astype(jnp.bfloat16)
    mixed = jnp.einsum("rshgj,rjhd->rshgd", prob_old, cached_v, preferred_element_type=jnp.float32)
    mixed = mixed + jnp.einsum(
        "rshgt,rthd->rshgd", prob_new, dec_v, preferred_element_type=jnp.float32
    )
    return mixed.reshape(rows, 2, q_cols).astype(jnp.bfloat16)


def on_device(
    tokens,
    token_ids,
    out_grad,
    w_query,
    w_key,
    w_value,
    dec_states,
    cache_lens,
    key_cache,
    value_cache,
):
    q_cols = w_query.shape[1]
    kv_cols = w_key.shape[1]
    average = 1.0 / lax.axis_size("fsdp")
    shard = jnp.concatenate([w_query, w_key, w_value], 1)
    gathered = lax.all_gather(shard, "fsdp", axis=0, tiled=True)
    acts = local_grads(tokens, token_ids, out_grad, gathered, q_cols, kv_cols)
    partial_input = lax.dot_general(
        acts, gathered, (((1,), (1,)), ((), ())), preferred_element_type=jnp.float32
    )
    input_grad = lax.psum_scatter(partial_input, "tensor", scatter_dimension=1, tiled=True).astype(
        jnp.bfloat16
    )
    grad_sum = lax.psum_scatter(
        lax.dot_general(tokens, acts, (((0,), (0,)), ((), ())), preferred_element_type=jnp.float32),
        "fsdp",
        scatter_dimension=0,
        tiled=True,
    )
    grad_cat = (grad_sum * average).astype(jnp.bfloat16)
    fresh = (shard.astype(jnp.float32) - learn_rate * grad_cat.astype(jnp.float32)).astype(
        jnp.bfloat16
    )
    fresh_full = lax.all_gather(fresh, "fsdp", axis=0, tiled=True)
    grad_query = grad_cat[:, :q_cols]
    grad_key = grad_cat[:, q_cols : q_cols + kv_cols]
    grad_value = grad_cat[:, q_cols + kv_cols :]
    dec_out = decode_steps(
        dec_states, cache_lens, key_cache, value_cache, fresh_full, q_cols, kv_cols
    )
    return (grad_query, grad_key, grad_value, input_grad, dec_out)


def solution(mesh):
    placed = (
        P("fsdp", None),
        P("fsdp"),
        P("fsdp", "tensor"),
        P("fsdp", "tensor"),
        P("fsdp", "tensor"),
        P("fsdp", "tensor"),
        P("fsdp", None, None),
        P("fsdp"),
        P("fsdp", None, "tensor"),
        P("fsdp", None, "tensor"),
    )
    return jax.shard_map(
        on_device,
        mesh=mesh,
        in_specs=placed,
        out_specs=(
            P("fsdp", "tensor"),
            P("fsdp", "tensor"),
            P("fsdp", "tensor"),
            P("fsdp", "tensor"),
            P("fsdp", None, "tensor"),
        ),
        check_vma=False,
    )
```

profile of v0, /device:TPU:1, one launch (start us, length us, event | category | flops | bytes accessed | tf_op | source)
XLA Modules:
  0.0 405.4 jit_solution(14857315165301284014)
XLA Ops:
  7.2 0.0 all-gather.3.cloned.1.call-start
  7.2 0.9 copy.94
  8.2 0.9 copy.95
  9.1 1.1 copy.93
  10.2 0.8 pad_maximum_fusion.1
  11.0 0.0 all-gather.3.cloned.1.call-update
  11.0 0.0 reduce-scatter.3.cloned.1.call-start
  11.0 0.7 convert_bitcast_fusion
  11.7 0.3 reduce-window.9
  12.0 0.1 slice.35
  12.1 1.3 copy.128
  13.4 0.1 slice_reduce_fusion
  13.5 0.1 add_bitcast_fusion
  13.6 0.2 fusion.43
  13.8 67.9 %all-gather.3.cloned.1.call-done = bf16[4096,768]{0,1:T(8,128)(2,1)} async-done(((bf16[256,768]{0,1:T(8,128)(2,1)}), bf16[4096,768]{0,1:T(8,128)(2,1)}) %all-gather.3.cloned.1.call-update) | async-done | bytes 6291472 | tf_op jit(solution)/shard_map/all_gather | solution.py:108
  81.7 7.4 %fusion.28 = bf16[512,768]{0,1:T(8,128)(2,1)S(1)} fusion(bf16[4096,768]{0,1:T(8,128)(2,1)} %all-gather.3.cloned.1.call-done, bf16[512,4096]{1,0:T(8,128)(2,1)} %param.10), kind=kOutput, calls=%fused_computation.25 | convolution fusion | flops 3221618688 | bytes 11272192 | tf_op jit(solution)/shard_map/dot_general | solution.py:20
  89.2 0.9 fusion.10
  90.1 0.9 fusion.9
  91.0 1.4 fusion.32
  92.4 1.6 fusion.4
  94.0 1.5 fusion.23
  95.5 0.0 copy-start.2
  95.5 0.8 fusion.36
  96.3 0.4 convolution_convert_fusion.1
  96.8 0.9 copy-done.2
  97.7 6.4 %convolution_bitcast_fusion = f32[4096,768]{0,1:T(8,128)} fusion(bf16[512,4096]{1,0:T(8,128)(2,1)S(1)} %copy-done.2, bf16[512,128]{0,1:T(8,128)(2,1)S(1)} %fusion.32, bf16[512,128]{0,1:T(8,128)(2,1)S(1)} %fusion.36, bf16[512,512]{0,1:T(8,128)(2,1)S(1)} %bitcast.178), kind=kOutput, calls=%fused_computation | convolution fusion | flops 3223584768 | bytes 17563648 | tf_op jit(solution)/shard_map/dot_general | solution.py:117
  104.0 0.0 reduce-scatter.3.cloned.1.call-update
  104.1 0.2 reduce-scatter.5.cloned.1.call-start
  104.3 8.4 %fusion.45 = f32[512,4096]{1,0:T(8,128)} fusion(bf16[4096,768]{0,1:T(8,128)(2,1)} %all-gather.3.cloned.1.call-done, bf16[512,128]{0,1:T(8,128)(2,1)S(1)} %fusion.32, bf16[512,128]{0,1:T(8,128)(2,1)S(1)} %fusion.36, bf16[512,512]{0,1:T(8,128)(2,1)S(1)} %bitcast.179), kind=kOutput, calls=%fused_computation.48 | convolution fusion | flops 3223584768 | bytes 15466496 | tf_op jit(solution)/shard_map/dot_general | solution.py:110
  112.7 0.0 copy-start
  112.7 0.0 copy-start.1
  112.7 0.0 reduce-scatter.5.cloned.1.call-update
  112.8 0.0 all-gather.5.cloned.1.call-start
  112.8 110.4 %reduce-scatter.3.cloned.1.call-done = f32[256,768]{0,1:T(8,128)} async-done(((f32[4096,768]{0,1:T(8,128)}), f32[256,768]{0,1:T(8,128)}) %reduce-scatter.3.cloned.1.call-update) | async-done | bytes 786448 | tf_op jit(solution)/shard_map/reduce_scatter | solution.py:116
  223.2 2.0 subtract_convert_fusion
  225.2 0.0 all-gather.5.cloned.1.call-update
  225.3 0.0 copy-done
  225.3 0.1 reshape.227
  225.3 0.0 copy-done.1
  225.3 0.1 iota_compare_fusion.1
  225.4 91.8 %reduce-scatter.5.cloned.1.call-done = f32[512,512]{1,0:T(8,128)} async-done(((f32[512,4096]{1,0:T(8,128)}), f32[512,512]{1,0:T(8,128)}) %reduce-scatter.5.cloned.1.call-update) | async-done | bytes 1048592 | tf_op jit(solution)/shard_map/reduce_scatter | solution.py:113
  317.2 2.1 convert_element_type.88
  319.4 0.8 copy.111
  320.2 0.7 copy.113
  320.9 0.7 copy.112
  321.7 63.8 %all-gather.5.cloned.1.call-done = bf16[4096,768]{0,1:T(8,128)(2,1)} async-done(((bf16[256,768]{0,1:T(8,128)(2,1)}), bf16[4096,768]{0,1:T(8,128)(2,1)}) %all-gather.5.cloned.1.call-update) | async-done | bytes 6291472 | tf_op jit(solution)/shard_map/all_gather | solution.py:126
  385.5 4.5 %fusion.41 = bf16[16,768]{1,0:T(8,128)(2,1)S(1)} fusion(bf16[4096,768]{0,1:T(8,128)(2,1)} %all-gather.5.cloned.1.call-done, bf16[16,4096]{1,0:T(8,128)(2,1)S(1)} %reshape.227), kind=kOutput, calls=%fused_computation.36 | convolution fusion | flops 100675584 | bytes 6447104 | tf_op jit(solution)/shard_map/dot_general | solution.py:63
  390.0 0.2 convolution_multiply_fusion
  390.3 0.1 copy.104
  390.4 3.5 fusion.59
  393.9 0.1 copy.105
  394.0 0.1 fusion.50
  394.1 0.1 fusion.51
  394.2 0.1 copy.106
  394.2 0.3 fusion.44
  394.6 0.1 copy.107
  394.7 0.1 fusion.52
  394.8 0.1 copy.108
  394.9 0.1 copy.110
  395.0 3.1 fusion.37
  398.0 0.2 fusion.42
  398.3 0.6 convert_element_type.99
  (10 shorter events, 0.1 us)
Async XLA Ops:
  7.2 74.5 %all-gather.3.cloned.1.call-start = ((), (), s32[]{:S(2)}) async-start(), calls=%async_computation.2 | async-start | bytes 6684672 | tf_op jit(solution)/shard_map/all_gather | solution.py:108
  11.0 212.2 %reduce-scatter.3.cloned.1.call-start = ((), (), s32[]{:S(2)}) async-start(), calls=%async_computation.3 | async-start | bytes 13369344 | tf_op jit(solution)/shard_map/reduce_scatter | solution.py:116
  95.5 2.2 copy-start.2
  104.1 213.2 %reduce-scatter.5.cloned.1.call-start = ((), (), s32[]{:S(2)}) async-start(), calls=%async_computation.4 | async-start | bytes 9437184 | tf_op jit(solution)/shard_map/reduce_scatter | solution.py:113
  112.7 112.5 %copy-start = (bf16[8,2,4096]{2,1,0:T(2,128)(2,1)S(1)}, bf16[8,2,4096]{2,1,0:T(2,128)(2,1)}, u32[]{:S(2)}) copy-start(bf16[8,2,4096]{2,1,0:T(2,128)(2,1)} %param.16) | copy-start | bytes 393220
  112.7 112.6 %copy-start.1 = (s32[8]{0:T(128)S(1)}, s32[8]{0:T(128)}, u32[]{:S(2)}) copy-start(s32[8]{0:T(128)} %param.17) | copy-start | bytes 100
  112.8 272.7 %all-gather.5.cloned.1.call-start = ((), (), s32[]{:S(2)}) async-start(), calls=%async_computation.5 | async-start | bytes 6684672 | tf_op jit(solution)/shard_map/all_gather | solution.py:126
Sparse Core Ops, SparseCore 0:
  11.1 70.5 all-gather.2
  104.2 118.9 reduce-scatter.2
  225.6 91.5 reduce-scatter.4
  319.4 66.0 all-gather.4
where the time goes:
time: 406 us; the launch traced here: 405 us
  waiting for transfers between devices  334 us (82%)
  matrix products  38.9 us (10%)
  between operations  14 us (3%)
  other arithmetic  9.27 us (2%)
  local copies, waits for them, and re-layouts  9 us (2%)
    reduce_scatter x1, waiting for transfers between devices, on_device(): lax.psum_scatter(lax.dot_general(tokens, acts, (((0,), (0,)), ((), ())),...  110 us
    reduce_scatter x1, waiting for transfers between devices, on_device(): lax.psum_scatter(partial_input, 'tensor', scatter_dimension=1, tiled=True)  91.8 us
    all_gather x1, waiting for transfers between devices, on_device(): gathered = lax.all_gather(shard, 'fsdp', axis=0, tiled=True)  67.9 us
    all_gather x1, waiting for transfers between devices, on_device(): fresh_full = lax.all_gather(fresh, 'fsdp', axis=0, tiled=True)  63.8 us
    dot_general x1, matrix products, on_device(): lax.dot_general(acts, gathered, (((1,), (1,)), ((), ())), preferred_eleme...  8.42 us
  transfers between devices with their start and end apart: 4, of which 4 were waited for; matrix products, arithmetic and copies ran while one was open for 4% of the time, Pallas kernels for 0%

commit v1 on v0

v1 whole, which is shorter than its diff:
```python
import math

import jax
import jax.numpy as jnp
from jax import lax
from jax.experimental import pallas as pl
from jax.experimental.pallas import tpu as pltpu
from jax.sharding import PartitionSpec as P

MESH = pl.DeviceIdType.MESH
BF = jnp.bfloat16
F32 = jnp.float32

HD = 128
LEARN_RATE = 0.004
BOS_ID = 128000
MASKED = -1e30

TOK = 512
D = 4096
QC = 512
COLS = 768
ROWS = 256
HALF = ROWS // 2
GROUPS = QC // HD
NF = 16
FEAT = 512
DEC = 16
CACHE = 2048
DROWS = 8

G_SIB = 0
G_P, G_M, G_X, G_PF, G_MF, G_P1, G_M1, G_XF = range(8, 16)
R_SIB = 16
R_X1, R_PQ, R_MQ, R_PB, R_MB, R_PF, R_MF, R_PA, R_MA, R_X2 = range(24, 34)
T_BASE = 34
T_PF, T_MF, T_PB, T_MB, T_PA, T_MA = range(6)
T_X = 46
D_IN = 47
D_OUT = 63
N_MSG = 79

L_TOK, L_OG, L_WQ, L_WK, L_WV, L_DEC, L_KC, L_VC, L_OWN, L_GQ, L_GK, L_GV, L_IG, L_DO, L_OWN2 = range(15)
N_LOCAL = 15

NT = (((1,), (1,)), ((), ()))


def f32_dot(a, b):
    return jnp.dot(a, b, preferred_element_type=F32)


def f32_dot_nt(a, b):
    return lax.dot_general(a, b, NT, preferred_element_type=F32)


def kernel(
    ids, lens, tok_h, og_h, wq_h, wk_h, wv_h, dec_h, kc_h, vc_h,
    gq_o, gk_o, gv_o, ig_o, do_o,
    tok, tok_t, w, proj, pb, og, bias, acts, key_t, gk_acc, gv_acc,
    sbs, acc, rx1, rx0, rm, rp, qm, qp, rfm, rfp,
    part, tfm, tfp, tm, tp, tx, ig, gout,
    kc, vc, dec, dec_in, dp, dpr, dout,
    ssem, rsem, lsem,
):
    f = lax.axis_index("fsdp")
    t = lax.axis_index("tensor")
    xh, z, c = f // 8, (f // 2) % 4, f % 2
    xl, y = t // 4, t % 4

    def fid(dx, dz, dc):
        return ((xh + dx) % 2) * 8 + ((z + dz) % 4) * 2 + (c + dc) % 2

    def tid(dx, dy):
        return ((xl + dx) % 2) * 4 + (y + dy) % 4

    sib = (fid(0, 0, 1), t)
    zp, zm, xp = (fid(0, 1, 0), t), (fid(0, 3, 0), t), (fid(1, 0, 0), t)
    yp, ym, xt = (f, tid(0, 1)), (f, tid(0, 3)), (f, tid(1, 0))

    def local(src, dst, i):
        return pltpu.make_async_copy(src, dst, lsem.at[i])

    sent = []

    def msg(i, src, dst, to):
        return pltpu.make_async_remote_copy(
            src_ref=src, dst_ref=dst, send_sem=ssem.at[i], recv_sem=rsem.at[i], device_id=to, device_id_type=MESH
        )

    def send(i, src, dst, to):
        m = msg(i, src, dst, to)
        m.start()
        sent.append(m)

    def arrived(i, ref, to):
        msg(i, ref, ref, to).wait_recv()

    def peer(k):
        return lax.rem(f + k, NF)

    own_w = w.at[f]
    loads = [
        local(wq_h, own_w.at[:, pl.ds(0, QC)], L_WQ),
        local(wk_h, own_w.at[:, pl.ds(QC, HD)], L_WK),
        local(wv_h, own_w.at[:, pl.ds(QC + HD, HD)], L_WV),
    ]
    for m in loads:
        m.start()
    load_dec = local(dec_h, dec, L_DEC)
    load_dec.start()
    load_tok = local(tok_h, tok, L_TOK)
    load_tok.start()
    load_og = local(og_h, og, L_OG)
    load_og.start()

    barrier = pltpu.get_barrier_semaphore()
    for k in range(1, NF):
        pl.semaphore_signal(barrier, inc=1, device_id=(peer(k), t), device_id_type=MESH)
    for to in (yp, ym, xt):
        pl.semaphore_signal(barrier, inc=1, device_id=to, device_id_type=MESH)
    for m in loads:
        m.wait()
    pl.semaphore_wait(barrier, NF + 2)

    send(G_P, own_w, own_w, zp)
    send(G_M, own_w, own_w, zm)
    send(G_X, own_w, own_w, xp)
    send(G_SIB, own_w, own_w, sib)

    load_dec.wait()

    def dec_piece(k):
        to = peer(k)
        return msg(
            D_IN + k,
            dec.at[:, pl.ds(pl.multiple_of(to * ROWS, ROWS), ROWS)],
            dec_in.at[pl.ds(pl.multiple_of(f * DEC, DEC), DEC), :],
            (to, t),
        )

    def send_dec(k, carry):
        dec_piece(k).start()
        return carry

    lax.fori_loop(1, NF, send_dec, 0)
    own_dec = local(
        dec.at[:, pl.ds(pl.multiple_of(f * ROWS, ROWS), ROWS)],
        dec_in.at[pl.ds(pl.multiple_of(f * DEC, DEC), DEC), :],
        L_OWN,
    )
    own_dec.start()
    load_kc = local(kc_h, kc, L_KC)
    load_vc = local(vc_h, vc, L_VC)
    load_kc.start()
    load_vc.start()

    bos = (ids[...] == BOS_ID).astype(F32)
    row = lax.broadcasted_iota(jnp.int32, (TOK, TOK), 0)
    col = lax.broadcasted_iota(jnp.int32, (TOK, TOK), 1)
    seg_row = f32_dot(jnp.broadcast_to(bos, (16, TOK)).astype(BF), (row <= col).astype(BF))
    seg_col = f32_dot_nt((col <= row).astype(BF), jnp.broadcast_to(bos, (HD, TOK)).astype(BF))
    seg_col = jnp.concatenate([seg_col] * (TOK // HD), axis=1)
    bias[...] = jnp.where((row <= col) & (seg_col == seg_row[0:1, :]), 0.0, MASKED)

    load_tok.wait()

    def turn(i, carry):
        at = pl.ds(pl.multiple_of(i * ROWS, ROWS), ROWS)
        tok_t[at, :] = tok[:, at].T
        return carry

    lax.fori_loop(0, NF, turn, 0)

    def project(dx, dz, first=False):
        chip = fid(dx, dz, 0) // 2
        at = pl.ds(pl.multiple_of(chip * 2 * ROWS, 2 * ROWS), 2 * ROWS)
        rows = w[pl.ds(chip * 2, 2)].reshape(2 * ROWS, COLS)
        term = f32_dot(tok[:, at], rows)
        proj[...] = term if first else proj[...] + term

    def shard(dx, dz, dc=0):
        return w.at[fid(dx, dz, dc)]

    def pass_on(dx, dz):
        send(G_SIB + dx * 4 + dz, shard(dx, dz), shard(dx, dz), sib)

    def from_sib(dx, dz):
        arrived(G_SIB + dx * 4 + dz, shard(dx, dz, 1), sib)

    from_sib(0, 0)
    project(0, 0, True)

    top, bottom = pl.ds(0, HALF), pl.ds(HALF, HALF)
    arrived(G_P, shard(0, 3), zp)
    send(G_PF, shard(0, 3).at[top], shard(0, 3).at[top], zp)
    arrived(G_M, shard(0, 1), zm)
    send(G_MF, shard(0, 1).at[bottom], shard(0, 1).at[bottom], zm)
    arrived(G_X, shard(1, 0), xp)
    send(G_P1, shard(1, 0), shard(1, 0), zp)
    send(G_M1, shard(1, 0), shard(1, 0), zm)
    pass_on(0, 3)
    pass_on(0, 1)
    pass_on(1, 0)
    for at in ((0, 3), (0, 1), (1, 0)):
        from_sib(*at)
        project(*at)
    arrived(G_PF, shard(0, 2).at[top], zp)
    arrived(G_MF, shard(0, 2).at[bottom], zm)
    send(G_XF, shard(0, 2), shard(0, 2), xp)
    pass_on(0, 2)
    from_sib(0, 2)
    project(0, 2)
    arrived(G_P1, shard(1, 3), zp)
    pass_on(1, 3)
    arrived(G_M1, shard(1, 1), zm)
    pass_on(1, 1)
    from_sib(1, 3)
    project(1, 3)
    from_sib(1, 1)
    project(1, 1)
    arrived(G_XF, shard(1, 2), xp)
    pass_on(1, 2)
    from_sib(1, 2)
    project(1, 2)

    pb[...] = proj[...].astype(BF)
    load_og.wait()
    key_t[...] = pb[:, QC:QC + HD].T
    gk_acc[...] = jnp.zeros_like(gk_acc)
    gv_acc[...] = jnp.zeros_like(gv_acc)
    scale = 1.0 / math.sqrt(HD)
    width = TOK // 2

    def head(h, carry):
        at = pl.ds(pl.multiple_of(h * HD, HD), HD)
        for block in range(2):
            qs = pl.ds(block * width, width)
            seen = (block + 1) * width
            ks = pl.ds(0, seen)
            keys = pb[ks, pl.ds(QC, HD)]
            values = pb[ks, pl.ds(QC + HD, HD)]
            query = pb[qs, at]
            upstream = og[qs, at]
            scores = f32_dot_nt(keys, query) * scale + bias[ks, qs]
            expo = jnp.exp(scores - jnp.max(scores, 0, keepdims=True))
            probs = expo * (1.0 / jnp.sum(expo, 0, keepdims=True))
            dprob = f32_dot_nt(values, upstream)
            delta = jnp.sum(probs * dprob, 0, keepdims=True)
            dscore = (probs * (dprob - delta) * scale).astype(BF)
            gv_acc[ks, :] += f32_dot(probs.astype(BF), upstream)
            gk_acc[ks, :] += f32_dot(dscore, query)
            acts[qs, at] = f32_dot(key_t[:, ks], dscore).T.astype(BF)
        return carry

    lax.fori_loop(0, GROUPS, head, 0)
    acts[:, QC:QC + HD] = gk_acc[...].astype(BF)
    acts[:, QC + HD:] = gv_acc[...].astype(BF)

    def grad_block(slot):
        rows = tok_t[pl.ds(pl.multiple_of(slot * ROWS, ROWS), ROWS), :]
        return f32_dot(rows, acts[...])

    def chip_of(i):
        return i // 4, i % 4

    def to_sib(i):
        return msg(R_SIB + i, sbs.at[i], acc.at[i], sib)

    def sib_block(k, carry):
        i = 7 - k
        dx, dz = chip_of(i)
        sbs[i] = grad_block(fid(dx, dz, 1)).astype(BF)
        to_sib(i).start()
        return carry

    def own_block(i, carry):
        dx, dz = chip_of(i)
        block = grad_block(fid(dx, dz, 0))
        arrived(R_SIB + i, acc.at[i], sib)
        acc[i] = (block + acc[i].astype(F32)).astype(BF)
        return carry

    def add(dst, *terms):
        total = dst[...].astype(F32)
        for x in terms:
            total = total + x[...].astype(F32)
        dst[...] = total.astype(BF)

    lax.fori_loop(0, 8, sib_block, 0)
    lax.fori_loop(4, 8, own_block, 0)
    send(R_X1, acc.at[6], rx1, xp)
    send(R_PQ, acc.at[5], qm, zp)
    send(R_MQ, acc.at[7], qp, zm)
    lax.fori_loop(0, 4, own_block, 0)
    send(R_PB, acc.at[1, bottom], rm.at[bottom], zp)
    send(R_MB, acc.at[3, top], rp.at[top], zm)

    t_top, t_bottom = pl.ds(0, TOK // 2), pl.ds(TOK // 2, TOK // 2)

    def input_block(i, carry):
        dx, dy = chip_of(i)
        rows = w[pl.ds(tid(dx, dy) * 2, 2)].reshape(2 * ROWS, COLS)
        part[i] = f32_dot_nt(acts[...], rows).astype(BF)
        return carry

    def send_near(dx):
        base, i = T_BASE + dx * 6, dx * 4
        send(base + T_PF, part.at[i + 2, t_top], tfp.at[dx], yp)
        send(base + T_MF, part.at[i + 2, t_bottom], tfm.at[dx], ym)
        send(base + T_PB, part.at[i + 1, t_bottom], tm.at[dx, t_bottom], yp)
        send(base + T_MB, part.at[i + 3, t_top], tp.at[dx, t_top], ym)

    def send_relayed(dx):
        base, i = T_BASE + dx * 6, dx * 4
        arrived(base + T_PF, tfp.at[dx], yp)
        add(part.at[i + 1, t_top], tfp.at[dx])
        send(base + T_PA, part.at[i + 1, t_top], tm.at[dx, t_top], yp)
        arrived(base + T_MF, tfm.at[dx], ym)
        add(part.at[i + 3, t_bottom], tfm.at[dx])
        send(base + T_MA, part.at[i + 3, t_bottom], tp.at[dx, t_bottom], ym)

    def ring_arrived(dx):
        base = T_BASE + dx * 6
        arrived(base + T_PB, tm.at[dx, t_bottom], yp)
        arrived(base + T_MB, tp.at[dx, t_top], ym)
        arrived(base + T_PA, tm.at[dx, t_top], yp)
        arrived(base + T_MA, tp.at[dx, t_bottom], ym)

    lax.fori_loop(4, 8, input_block, 0)
    send_near(1)
    lax.fori_loop(0, 4, input_block, 0)

    arrived(R_X1, rx1, xp)
    add(acc.at[2], rx1)
    send(R_PF, acc.at[2, top], rfp, zp)
    send(R_MF, acc.at[2, bottom], rfm, zm)
    arrived(R_PQ, qm, zp)
    arrived(R_MQ, qp, zm)
    add(acc.at[4], qm, qp)
    send(R_X2, acc.at[4], rx0, xp)
    send_relayed(1)
    send_near(0)
    arrived(R_PF, rfp, zp)
    add(acc.at[1, top], rfp)
    send(R_PA, acc.at[1, top], rm.at[top], zp)
    arrived(R_MF, rfm, zm)
    add(acc.at[3, bottom], rfm)
    send(R_MA, acc.at[3, bottom], rp.at[bottom], zm)
    ring_arrived(1)
    add(part.at[4], tm.at[1], tp.at[1])
    send(T_X, part.at[4], tx, xt)
    send_relayed(0)

    arrived(R_PB, rm.at[bottom], zp)
    arrived(R_MB, rp.at[top], zm)
    arrived(R_PA, rm.at[top], zp)
    arrived(R_MA, rp.at[bottom], zm)
    arrived(R_X2, rx0, xp)
    total = acc[0].astype(F32) + rm[...].astype(F32) + rp[...].astype(F32) + rx0[...].astype(F32)
    grad = (total * (1.0 / NF)).astype(BF)
    gout[...] = grad
    stores = [
        local(gout.at[:, pl.ds(0, QC)], gq_o, L_GQ),
        local(gout.at[:, pl.ds(QC, HD)], gk_o, L_GK),
        local(gout.at[:, pl.ds(QC + HD, HD)], gv_o, L_GV),
    ]
    for m in stores:
        m.start()
    fresh = (own_w[...].astype(F32) - LEARN_RATE * grad.astype(F32)).astype(BF)

    def dec_arrived(k, carry):
        at = pl.ds(pl.multiple_of(peer(NF - k) * DEC, DEC), DEC)
        arrived(D_IN + k, dec_in.at[at, :], (peer(k), t))
        return carry

    lax.fori_loop(1, NF, dec_arrived, 0)
    own_dec.wait()
    dp[...] = f32_dot(dec_in[...], fresh).astype(BF)

    def dec_out_piece(k):
        to = peer(k)
        return msg(
            D_OUT + k,
            dp.at[pl.ds(pl.multiple_of(to * DEC, DEC), DEC), :],
            dpr.at[pl.ds(pl.multiple_of(f * DEC, DEC), DEC), :],
            (to, t),
        )

    def send_dec_out(k, carry):
        dec_out_piece(k).start()
        return carry

    lax.fori_loop(1, NF, send_dec_out, 0)
    own_rows = pl.ds(pl.multiple_of(f * DEC, DEC), DEC)
    own_part = local(dp.at[own_rows, :], dpr.at[own_rows, :], L_OWN2)
    own_part.start()
    load_kc.wait()
    load_vc.wait()

    def dec_out_arrived(k, carry):
        at = pl.ds(pl.multiple_of(peer(NF - k) * DEC, DEC), DEC)
        arrived(D_OUT + k, dpr.at[at, :], (peer(k), t))
        return carry

    lax.fori_loop(1, NF, dec_out_arrived, 0)
    own_part.wait()
    dsum = dpr[0:DEC, :].astype(F32)
    for k in range(1, NF):
        dsum = dsum + dpr[k * DEC:(k + 1) * DEC, :].astype(F32)
    dsum = dsum.astype(BF)

    dec_q = dsum[:, :QC].astype(F32)
    dec_k = dsum[:, QC:QC + HD]
    dec_v = dsum[:, QC + HD:]
    n_q = 2 * GROUPS
    place = lax.broadcasted_iota(jnp.int32, (n_q, CACHE), 1)
    new_col = lax.broadcasted_iota(jnp.int32, (n_q, DEC), 1)
    new_step = lax.broadcasted_iota(jnp.int32, (n_q, DEC), 0) % 2
    for r in range(DROWS):
        q = jnp.concatenate([dec_q[2 * r:2 * r + 2, g * HD:(g + 1) * HD] for g in range(GROUPS)], axis=0).astype(BF)
        older = jnp.where(place < lens[r], f32_dot_nt(q, kc[r]) * scale, MASKED)
        visible = (new_col // 2 == r) & (new_col % 2 <= new_step)
        newer = jnp.where(visible, f32_dot_nt(q, dec_k) * scale, MASKED)
        best = jnp.maximum(jnp.max(older, 1, keepdims=True), jnp.max(newer, 1, keepdims=True))
        exp_old = jnp.exp(older - best)
        exp_new = jnp.exp(newer - best)
        inv = 1.0 / (jnp.sum(exp_old, 1, keepdims=True) + jnp.sum(exp_new, 1, keepdims=True))
        mixed = f32_dot((exp_old * inv).astype(BF), vc[r]) + f32_dot((exp_new * inv).astype(BF), dec_v)
        for g in range(GROUPS):
            dout[2 * r:2 * r + 2, g * HD:(g + 1) * HD] = mixed[2 * g:2 * g + 2, :]
    do_o[...] = dout[...].astype(BF)

    ring_arrived(0)
    arrived(T_X, tx, xt)
    total = part[0].astype(F32) + tm[0].astype(F32) + tp[0].astype(F32) + tx[...].astype(F32)
    ig[...] = total.astype(BF)
    store_ig = local(ig, ig_o, L_IG)
    store_ig.start()
    stores.append(store_ig)

    for m in sent:
        m.wait_send()

    def sent_small(k, carry):
        dec_piece(k).wait_send()
        dec_out_piece(k).wait_send()
        return carry

    lax.fori_loop(1, NF, sent_small, 0)

    def sent_sib(i, carry):
        to_sib(i).wait_send()
        return carry

    lax.fori_loop(0, 8, sent_sib, 0)
    for m in stores:
        m.wait()


def on_device(tokens, token_ids, out_grad, w_query, w_key, w_value, dec_states, cache_lens, key_cache, value_cache):
    anywhere = pl.BlockSpec(memory_space=pl.ANY)
    vmem = pl.BlockSpec(memory_space=pltpu.VMEM)

    def buf(*shape, dtype=BF):
        return pltpu.VMEM(shape, dtype)

    shapes = [(ROWS, QC), (ROWS, HD), (ROWS, HD), (TOK, FEAT), (DEC, QC)]
    *grads, dec_out = pl.pallas_call(
        kernel,
        out_shape=[jax.ShapeDtypeStruct(s, BF) for s in shapes],
        in_specs=[vmem, pl.BlockSpec(memory_space=pltpu.SMEM)] + [anywhere] * 8,
        out_specs=[anywhere] * 4 + [vmem],
        scratch_shapes=[
            buf(TOK, D), buf(D, TOK), buf(NF, ROWS, COLS), buf(TOK, COLS, dtype=F32), buf(TOK, COLS), buf(TOK, QC),
            buf(TOK, TOK, dtype=F32), buf(TOK, COLS), buf(HD, TOK), buf(TOK, HD, dtype=F32), buf(TOK, HD, dtype=F32),
            buf(8, ROWS, COLS), buf(8, ROWS, COLS),
            buf(ROWS, COLS), buf(ROWS, COLS), buf(ROWS, COLS), buf(ROWS, COLS), buf(ROWS, COLS), buf(ROWS, COLS),
            buf(HALF, COLS), buf(HALF, COLS),
            buf(8, TOK, FEAT), buf(2, TOK // 2, FEAT), buf(2, TOK // 2, FEAT), buf(2, TOK, FEAT), buf(2, TOK, FEAT),
            buf(TOK, FEAT), buf(TOK, FEAT), buf(ROWS, COLS),
            buf(DROWS, CACHE, HD), buf(DROWS, CACHE, HD),
            buf(DEC, D), buf(NF * DEC, ROWS), buf(NF * DEC, COLS), buf(NF * DEC, COLS), buf(DEC, QC, dtype=F32),
            pltpu.SemaphoreType.DMA((N_MSG,)), pltpu.SemaphoreType.DMA((N_MSG,)), pltpu.SemaphoreType.DMA((N_LOCAL,)),
        ],
        compiler_params=pltpu.CompilerParams(collective_id=0, has_side_effects=True, vmem_limit_bytes=60 << 20),
        cost_estimate=pl.CostEstimate(flops=13 * 10**9, bytes_accessed=16 * 10**6, transcendentals=2 * 10**6),
    )(
        token_ids.reshape(1, TOK), cache_lens, tokens, out_grad, w_query, w_key, w_value,
        dec_states.reshape(DEC, D), key_cache, value_cache,
    )
    return (*grads, dec_out.reshape(DROWS, 2, QC))


def solution(mesh):
    placed = (
        P("fsdp", None),
        P("fsdp"),
        P("fsdp", "tensor"),
        P("fsdp", "tensor"),
        P("fsdp", "tensor"),
        P("fsdp", "tensor"),
        P("fsdp", None, None),
        P("fsdp"),
        P("fsdp", None, "tensor"),
        P("fsdp", None, "tensor"),
    )
    return jax.shard_map(
        on_device,
        mesh=mesh,
        in_specs=placed,
        out_specs=(
            P("fsdp", "tensor"),
            P("fsdp", "tensor"),
            P("fsdp", "tensor"),
            P("fsdp", "tensor"),
            P("fsdp", None, "tensor"),
        ),
        check_vma=False,
    )
```

time: 406 us -> 109 us (0.27)
  waiting for transfers between devices: 334 us -> 0 us
  Pallas kernels: 0 us -> 98.2 us
  matrix products: 38.9 us -> 0 us
  between operations: 14 us -> 0.64 us
  other arithmetic: 9.27 us -> 0 us
    reduce_scatter x2 -> x0, waiting for transfers between devices: 202 us -> none  [the longest x1 110 us: on_device(): lax.psum_scatter(lax.dot_general(tokens, acts, (((0,), (0,)), ((), ())),...]
    all_gather x2 -> x0, waiting for transfers between devices: 132 us -> none  [the longest x1 67.9 us: on_device(): gathered = lax.all_gather(shard, 'fsdp', axis=0, tiled=True)]
    pallas_call x0 -> x1, Pallas kernels: none -> 98.2 us  [on_device(): pl.pallas_call(kernel, out_shape=[jax.ShapeDtypeStruct(s, BF) for s in sh...]
    dot_general x13 -> x0, matrix products: 38.9 us -> none  [the longest x1 8.42 us: on_device(): lax.dot_general(acts, gathered, (((1,), (1,)), ((), ())), preferred_eleme...]
    convert_element_type x2 -> x0, other arithmetic: 4.1 us -> none  [the longest x1 2.08 us: on_device(): lax.psum_scatter(partial_input, 'tensor', scatter_dimension=1, tiled=True)]
  transfers between devices with their start and end apart: 4 -> 0, of which waited for: 4 -> 0; matrix products, arithmetic and copies ran while one was open for 4% -> 0% of each run, Pallas kernels for 0% -> 0%
where the time goes in v1:
time: 109 us; the launch traced here: 108 us
  Pallas kernels  98.2 us (90%)
  local copies, waits for them, and re-layouts  9.43 us (9%)
    pallas_call x1, Pallas kernels, on_device(): pl.pallas_call(kernel, out_shape=[jax.ShapeDtypeStruct(s, BF) for s in sh...  98.2 us
    unnamed x4, local copies, waits for them, and re-layouts  6.48 us

profile of v1, /device:TPU:1, one launch (start us, length us, event | category | flops | bytes accessed | tf_op | source)
XLA Modules:
  0.0 108.2 jit_solution(8075038114109357604)
XLA Ops:
  0.6 1.6 %reshape.20.dec_h = bf16[16,4096]{1,0:T(8,128)(2,1)} reshape(bf16[8,2,4096]{2,1,0:T(2,128)(2,1)} %param.16) | data formatting | bytes 262144 | tf_op jit(solution)/shard_map/reshape | solution.py:490
  2.2 98.2 %shard_map.137 = (bf16[256,512]{1,0:T(8,128)(2,1)}, bf16[256,128]{1,0:T(8,128)(2,1)}, bf16[256,128]{1,0:T(8,128)(2,1)}, bf16[512,512]{1,0:T(8,128)(2,1)}, bf16[16,512]{1,0:T(8,128)(2,1)}) custom-call(s32[1,512]{1,0:T(1,128)} %bitcast.1, s32[8]{0:T(128)} %lens.1, bf16[512,4096]{1,0:T(8,128)(2,1)} %tok_h.1, bf16[512,512]{1,0:T(8,128)(2,1)} %og_h.1, ...), custom_call_target="tpu_custom_call" | custom-call | flops 12999999488 | bytes 16000000 | tf_op jit(solution)/shard_map/pallas_call | solution.py:469
  100.4 1.3 %reshape.21 = bf16[8,2,512]{2,1,0:T(2,128)(2,1)} reshape(bf16[16,512]{1,0:T(8,128)(2,1)} %get-tuple-element.14) | data formatting | bytes 32768 | tf_op jit(solution)/shard_map/reshape | solution.py:492
  101.7 1.7 %copy.19 = bf16[256,512]{1,0:T(8,128)(2,1)} copy(bf16[256,512]{1,0:T(8,128)(2,1)} %get-tuple-element.20) | data formatting | bytes 524288
  103.4 1.5 %copy.20 = bf16[256,128]{1,0:T(8,128)(2,1)} copy(bf16[256,128]{1,0:T(8,128)(2,1)} %get-tuple-element.21) | data formatting | bytes 131072
  104.9 1.5 %copy.21 = bf16[256,128]{1,0:T(8,128)(2,1)} copy(bf16[256,128]{1,0:T(8,128)(2,1)} %get-tuple-element.22) | data formatting | bytes 131072
  106.4 1.9 %copy.22 = bf16[512,512]{1,0:T(8,128)(2,1)} copy(bf16[512,512]{1,0:T(8,128)(2,1)} %get-tuple-element.23) | data formatting | bytes 1048576

commit v2 on v1

--- a/solution.py
+++ b/solution.py
@@ -30,15 +30,15 @@
 DROWS = 8
 
 G_SIB = 0
-G_P, G_M, G_X, G_PF, G_MF, G_P1, G_M1, G_XF = range(8, 16)
-R_SIB = 16
-R_X1, R_PQ, R_MQ, R_PB, R_MB, R_PF, R_MF, R_PA, R_MA, R_X2 = range(24, 34)
-T_BASE = 34
+G_PT, G_PB, G_MT, G_MB, G_X, G_PF, G_MF, G_XA, G_XB, G_P1, G_M1, G_P2, G_M2 = range(8, 21)
+R_SIB = 21
+R_X1T, R_X1B, R_PQ, R_MQ, R_PB, R_MB, R_PF, R_MF, R_PA, R_MA, R_X2 = range(29, 40)
+T_BASE = 40
 T_PF, T_MF, T_PB, T_MB, T_PA, T_MA = range(6)
-T_X = 46
-D_IN = 47
-D_OUT = 63
-N_MSG = 79
+T_X = 52
+D_IN = 53
+D_OUT = 69
+N_MSG = 85
 
 L_TOK, L_OG, L_WQ, L_WK, L_WV, L_DEC, L_KC, L_VC, L_OWN, L_GQ, L_GK, L_GV, L_IG, L_DO, L_OWN2 = range(15)
 N_LOCAL = 15
@@ -60,7 +60,7 @@
     tok, tok_t, w, proj, pb, og, bias, acts, key_t, gk_acc, gv_acc,
     sbs, acc, rx1, rx0, rm, rp, qm, qp, rfm, rfp,
     part, tfm, tfp, tm, tp, tx, ig, gout,
-    kc, vc, dec, dec_in, dp, dpr, dout,
+    kc, vc, dec3, dec_f32, dec, dec_in, dp, dpr,
     ssem, rsem, lsem,
 ):
     f = lax.axis_index("fsdp")
@@ -68,8 +68,13 @@
     xh, z, c = f // 8, (f // 2) % 4, f % 2
     xl, y = t // 4, t % 4
 
+    sense = 1 + 2 * c
+
     def fid(dx, dz, dc):
-        return ((xh + dx) % 2) * 8 + ((z + dz) % 4) * 2 + (c + dc) % 2
+        return ((xh + dx) % 2) * 8 + ((z + sense * dz) % 4) * 2 + (c + dc) % 2
+
+    def place_of(dx, dz):
+        return dx * 4 + (sense * dz) % 4
 
     def tid(dx, dy):
         return ((xl + dx) % 2) * 4 + (y + dy) % 4
@@ -99,6 +104,10 @@
     def peer(k):
         return lax.rem(f + k, NF)
 
+    near = (sib, zp, zm, xp, yp, ym, xt)
+    barrier = pltpu.get_barrier_semaphore()
+    for to in near:
+        pl.semaphore_signal(barrier, inc=1, device_id=to, device_id_type=MESH)
     own_w = w.at[f]
     loads = [
         local(wq_h, own_w.at[:, pl.ds(0, QC)], L_WQ),
@@ -107,28 +116,118 @@
     ]
     for m in loads:
         m.start()
-    load_dec = local(dec_h, dec, L_DEC)
-    load_dec.start()
     load_tok = local(tok_h, tok, L_TOK)
     load_tok.start()
+    load_dec = local(dec_h, dec3, L_DEC)
+    load_dec.start()
     load_og = local(og_h, og, L_OG)
     load_og.start()
 
-    barrier = pltpu.get_barrier_semaphore()
-    for k in range(1, NF):
-        pl.semaphore_signal(barrier, inc=1, device_id=(peer(k), t), device_id_type=MESH)
-    for to in (yp, ym, xt):
-        pl.semaphore_signal(barrier, inc=1, device_id=to, device_id_type=MESH)
     for m in loads:
         m.wait()
-    pl.semaphore_wait(barrier, NF + 2)
-
-    send(G_P, own_w, own_w, zp)
-    send(G_M, own_w, own_w, zm)
+    pl.semaphore_wait(barrier, len(near))
+
+    top, bottom = pl.ds(0, HALF), pl.ds(HALF, HALF)
+    send(G_PT, own_w.at[top], own_w.at[top], zp)
+    send(G_MB, own_w.at[bottom], own_w.at[bottom], zm)
     send(G_X, own_w, own_w, xp)
-    send(G_SIB, own_w, own_w, sib)
+    send(G_PB, own_w.at[bottom], own_w.at[bottom], zp)
+    send(G_MT, own_w.at[top], own_w.at[top], zm)
+    send(G_SIB + place_of(0, 0), own_w, own_w, sib)
+
+    load_kc = local(kc_h, kc, L_KC)
+    load_vc = local(vc_h, vc, L_VC)
+    load_kc.start()
+    load_vc.start()
+
+    bos = (ids[...] == BOS_ID).astype(F32)
+    row = lax.broadcasted_iota(jnp.int32, (TOK, TOK), 0)
+    col = lax.broadcasted_iota(jnp.int32, (TOK, TOK), 1)
+    seg_row = f32_dot(jnp.broadcast_to(bos, (16, TOK)).astype(BF), (row <= col).astype(BF))
+    seg_col = f32_dot_nt((col <= row).astype(BF), jnp.broadcast_to(bos, (HD, TOK)).astype(BF))
+    seg_col = jnp.concatenate([seg_col] * (TOK // HD), axis=1)
+    bias[...] = jnp.where((row <= col) & (seg_col == seg_row[0:1, :]), 0.0, MASKED)
 
     load_dec.wait()
+    for r in range(DROWS):
+        dec_f32[2 * r:2 * r + 2, :] = dec3[r].astype(F32)
+    dec[...] = dec_f32[...].astype(BF)
+    load_tok.wait()
+
+    def turn(i, carry):
+        at = pl.ds(pl.multiple_of(i * ROWS, ROWS), ROWS)
+        tok_t[at, :] = tok[:, at].T
+        return carry
+
+    def project(dx, dz, first=False):
+        chip = fid(dx, dz, 0) // 2
+        at = pl.ds(pl.multiple_of(chip * 2 * ROWS, 2 * ROWS), 2 * ROWS)
+        rows = w[pl.ds(chip * 2, 2)].reshape(2 * ROWS, COLS)
+        term = f32_dot(tok[:, at], rows)
+        proj[...] = term if first else proj[...] + term
+
+    def shard(dx, dz, dc=0):
+        return w.at[fid(dx, dz, dc)]
+
+    def pass_on(dx, dz):
+        send(G_SIB + place_of(dx, dz), shard(dx, dz), shard(dx, dz), sib)
+
+    def from_sib(dx, dz):
+        arrived(G_SIB + place_of(dx, dz), shard(dx, dz, 1), sib)
+
+    def relay(i, ref, to):
+        send(i, ref, ref, to)
+
+    from_sib(0, 0)
+    project(0, 0, True)
+    lax.fori_loop(0, 4, turn, 0)
+
+    arrived(G_PT, shard(0, 3).at[top], zp)
+    relay(G_PF, shard(0, 3).at[top], zp)
+    relay(G_XA, shard(0, 3).at[top], xp)
+    arrived(G_MB, shard(0, 1).at[bottom], zm)
+    relay(G_MF, shard(0, 1).at[bottom], zm)
+    relay(G_XB, shard(0, 1).at[bottom], xp)
+    lax.fori_loop(4, 6, turn, 0)
+    arrived(G_X, shard(1, 0), xp)
+    relay(G_P1, shard(1, 0).at[bottom], zp)
+    relay(G_M1, shard(1, 0).at[top], zm)
+    pass_on(1, 0)
+    arrived(G_PB, shard(0, 3).at[bottom], zp)
+    pass_on(0, 3)
+    arrived(G_MT, shard(0, 1).at[top], zm)
+    pass_on(0, 1)
+    lax.fori_loop(6, 9, turn, 0)
+    from_sib(1, 0)
+    project(1, 0)
+    arrived(G_PF, shard(0, 2).at[top], zp)
+    arrived(G_MF, shard(0, 2).at[bottom], zm)
+    pass_on(0, 2)
+    arrived(G_XA, shard(1, 3).at[top], xp)
+    relay(G_P2, shard(1, 3).at[top], zp)
+    from_sib(0, 3)
+    project(0, 3)
+    from_sib(0, 1)
+    project(0, 1)
+    lax.fori_loop(9, 11, turn, 0)
+    arrived(G_XB, shard(1, 1).at[bottom], xp)
+    relay(G_M2, shard(1, 1).at[bottom], zm)
+    arrived(G_P1, shard(1, 3).at[bottom], zp)
+    pass_on(1, 3)
+    arrived(G_M1, shard(1, 1).at[top], zm)
+    pass_on(1, 1)
+    from_sib(0, 2)
+    project(0, 2)
+    lax.fori_loop(11, NF, turn, 0)
+    from_sib(1, 3)
+    project(1, 3)
+    from_sib(1, 1)
+    project(1, 1)
+    arrived(G_P2, shard(1, 2).at[top], zp)
+    arrived(G_M2, shard(1, 2).at[bottom], zm)
+    pass_on(1, 2)
+    from_sib(1, 2)
+    project(1, 2)
 
     def dec_piece(k):
         to = peer(k)
@@ -150,79 +249,6 @@
         L_OWN,
     )
     own_dec.start()
-    load_kc = local(kc_h, kc, L_KC)
-    load_vc = local(vc_h, vc, L_VC)
-    load_kc.start()
-    load_vc.start()
-
-    bos = (ids[...] == BOS_ID).astype(F32)
-    row = lax.broadcasted_iota(jnp.int32, (TOK, TOK), 0)
-    col = lax.broadcasted_iota(jnp.int32, (TOK, TOK), 1)
-    seg_row = f32_dot(jnp.broadcast_to(bos, (16, TOK)).astype(BF), (row <= col).astype(BF))
-    seg_col = f32_dot_nt((col <= row).astype(BF), jnp.broadcast_to(bos, (HD, TOK)).astype(BF))
-    seg_col = jnp.concatenate([seg_col] * (TOK // HD), axis=1)
-    bias[...] = jnp.where((row <= col) & (seg_col == seg_row[0:1, :]), 0.0, MASKED)
-
-    load_tok.wait()
-
-    def turn(i, carry):
-        at = pl.ds(pl.multiple_of(i * ROWS, ROWS), ROWS)
-        tok_t[at, :] = tok[:, at].T
-        return carry
-
-    lax.fori_loop(0, NF, turn, 0)
-
-    def project(dx, dz, first=False):
-        chip = fid(dx, dz, 0) // 2
-        at = pl.ds(pl.multiple_of(chip * 2 * ROWS, 2 * ROWS), 2 * ROWS)
-        rows = w[pl.ds(chip * 2, 2)].reshape(2 * ROWS, COLS)
-        term = f32_dot(tok[:, at], rows)
-        proj[...] = term if first else proj[...] + term
-
-    def shard(dx, dz, dc=0):
-        return w.at[fid(dx, dz, dc)]
-
-    def pass_on(dx, dz):
-        send(G_SIB + dx * 4 + dz, shard(dx, dz), shard(dx, dz), sib)
-
-    def from_sib(dx, dz):
-        arrived(G_SIB + dx * 4 + dz, shard(dx, dz, 1), sib)
-
-    from_sib(0, 0)
-    project(0, 0, True)
-
-    top, bottom = pl.ds(0, HALF), pl.ds(HALF, HALF)
-    arrived(G_P, shard(0, 3), zp)
-    send(G_PF, shard(0, 3).at[top], shard(0, 3).at[top], zp)
-    arrived(G_M, shard(0, 1), zm)
-    send(G_MF, shard(0, 1).at[bottom], shard(0, 1).at[bottom], zm)
-    arrived(G_X, shard(1, 0), xp)
-    send(G_P1, shard(1, 0), shard(1, 0), zp)
-    send(G_M1, shard(1, 0), shard(1, 0), zm)
-    pass_on(0, 3)
-    pass_on(0, 1)
-    pass_on(1, 0)
-    for at in ((0, 3), (0, 1), (1, 0)):
-        from_sib(*at)
-        project(*at)
-    arrived(G_PF, shard(0, 2).at[top], zp)
-    arrived(G_MF, shard(0, 2).at[bottom], zm)
-    send(G_XF, shard(0, 2), shard(0, 2), xp)
-    pass_on(0, 2)
-    from_sib(0, 2)
-    project(0, 2)
-    arrived(G_P1, shard(1, 3), zp)
-    pass_on(1, 3)
-    arrived(G_M1, shard(1, 1), zm)
-    pass_on(1, 1)
-    from_sib(1, 3)
-    project(1, 3)
-    from_sib(1, 1)
-    project(1, 1)
-    arrived(G_XF, shard(1, 2), xp)
-    pass_on(1, 2)
-    from_sib(1, 2)
-    project(1, 2)
 
     pb[...] = proj[...].astype(BF)
     load_og.wait()
@@ -261,25 +287,27 @@
         rows = tok_t[pl.ds(pl.multiple_of(slot * ROWS, ROWS), ROWS), :]
         return f32_dot(rows, acts[...])
 
-    def chip_of(i):
-        return i // 4, i % 4
+    def block_of(i, dc):
+        return ((xh + i // 4) % 2) * 8 + ((z + i % 4) % 4) * 2 + (c + dc) % 2
 
     def to_sib(i):
         return msg(R_SIB + i, sbs.at[i], acc.at[i], sib)
 
     def sib_block(k, carry):
         i = 7 - k
-        dx, dz = chip_of(i)
-        sbs[i] = grad_block(fid(dx, dz, 1)).astype(BF)
+        sbs[i] = grad_block(block_of(i, 1)).astype(BF)
         to_sib(i).start()
         return carry
 
     def own_block(i, carry):
-        dx, dz = chip_of(i)
-        block = grad_block(fid(dx, dz, 0))
+        block = grad_block(block_of(i, 0))
         arrived(R_SIB + i, acc.at[i], sib)
         acc[i] = (block + acc[i].astype(F32)).astype(BF)
         return carry
+
+    def sums(dx, dz, part=None):
+        ref = acc.at[place_of(dx, dz)]
+        return ref if part is None else ref.at[part]
 
     def add(dst, *terms):
         total = dst[...].astype(F32)
@@ -287,20 +315,10 @@
             total = total + x[...].astype(F32)
         dst[...] = total.astype(BF)
 
-    lax.fori_loop(0, 8, sib_block, 0)
-    lax.fori_loop(4, 8, own_block, 0)
-    send(R_X1, acc.at[6], rx1, xp)
-    send(R_PQ, acc.at[5], qm, zp)
-    send(R_MQ, acc.at[7], qp, zm)
-    lax.fori_loop(0, 4, own_block, 0)
-    send(R_PB, acc.at[1, bottom], rm.at[bottom], zp)
-    send(R_MB, acc.at[3, top], rp.at[top], zm)
-
     t_top, t_bottom = pl.ds(0, TOK // 2), pl.ds(TOK // 2, TOK // 2)
 
     def input_block(i, carry):
-        dx, dy = chip_of(i)
-        rows = w[pl.ds(tid(dx, dy) * 2, 2)].reshape(2 * ROWS, COLS)
+        rows = w[pl.ds(tid(i // 4, i % 4) * 2, 2)].reshape(2 * ROWS, COLS)
         part[i] = f32_dot_nt(acts[...], rows).astype(BF)
         return carry
 
@@ -327,26 +345,37 @@
         arrived(base + T_PA, tm.at[dx, t_top], yp)
         arrived(base + T_MA, tp.at[dx, t_bottom], ym)
 
+    lax.fori_loop(0, 8, sib_block, 0)
+    lax.fori_loop(4, 8, own_block, 0)
+    send(R_X1T, sums(1, 2, top), rx1.at[top], xp)
+    send(R_X1B, sums(1, 2, bottom), rx1.at[bottom], xp)
+    send(R_PQ, sums(1, 1), qm, zp)
+    send(R_MQ, sums(1, 3), qp, zm)
     lax.fori_loop(4, 8, input_block, 0)
     send_near(1)
+    lax.fori_loop(0, 4, own_block, 0)
     lax.fori_loop(0, 4, input_block, 0)
 
-    arrived(R_X1, rx1, xp)
-    add(acc.at[2], rx1)
-    send(R_PF, acc.at[2, top], rfp, zp)
-    send(R_MF, acc.at[2, bottom], rfm, zm)
+    arrived(R_X1T, rx1.at[top], xp)
+    add(sums(0, 2, top), rx1.at[top])
+    send(R_PF, sums(0, 2, top), rfp, zp)
+    send(R_PB, sums(0, 1, bottom), rm.at[bottom], zp)
+    send(R_MB, sums(0, 3, top), rp.at[top], zm)
+    send_relayed(1)
+    send_near(0)
+    arrived(R_X1B, rx1.at[bottom], xp)
+    add(sums(0, 2, bottom), rx1.at[bottom])
+    send(R_MF, sums(0, 2, bottom), rfm, zm)
     arrived(R_PQ, qm, zp)
     arrived(R_MQ, qp, zm)
-    add(acc.at[4], qm, qp)
-    send(R_X2, acc.at[4], rx0, xp)
-    send_relayed(1)
-    send_near(0)
+    add(sums(1, 0), qm, qp)
+    send(R_X2, sums(1, 0), rx0, xp)
     arrived(R_PF, rfp, zp)
-    add(acc.at[1, top], rfp)
-    send(R_PA, acc.at[1, top], rm.at[top], zp)
+    add(sums(0, 1, top), rfp)
+    send(R_PA, sums(0, 1, top), rm.at[top], zp)
     arrived(R_MF, rfm, zm)
-    add(acc.at[3, bottom], rfm)
-    send(R_MA, acc.at[3, bottom], rp.at[bottom], zm)
+    add(sums(0, 3, bottom), rfm)
+    send(R_MA, sums(0, 3, bottom), rp.at[bottom], zm)
     ring_arrived(1)
     add(part.at[4], tm.at[1], tp.at[1])
     send(T_X, part.at[4], tx, xt)
@@ -357,7 +386,7 @@
     arrived(R_PA, rm.at[top], zp)
     arrived(R_MA, rp.at[bottom], zm)
     arrived(R_X2, rx0, xp)
-    total = acc[0].astype(F32) + rm[...].astype(F32) + rp[...].astype(F32) + rx0[...].astype(F32)
+    total = sums(0, 0)[...].astype(F32) + rm[...].astype(F32) + rp[...].astype(F32) + rx0[...].astype(F32)
     grad = (total * (1.0 / NF)).astype(BF)
     gout[...] = grad
     stores = [
@@ -428,8 +457,7 @@
         inv = 1.0 / (jnp.sum(exp_old, 1, keepdims=True) + jnp.sum(exp_new, 1, keepdims=True))
         mixed = f32_dot((exp_old * inv).astype(BF), vc[r]) + f32_dot((exp_new * inv).astype(BF), dec_v)
         for g in range(GROUPS):
-            dout[2 * r:2 * r + 2, g * HD:(g + 1) * HD] = mixed[2 * g:2 * g + 2, :]
-    do_o[...] = dout[...].astype(BF)
+            do_o[2 * r:2 * r + 2, g * HD:(g + 1) * HD] = mixed[2 * g:2 * g + 2, :]
 
     ring_arrived(0)
     arrived(T_X, tx, xt)
@@ -458,6 +486,21 @@
         m.wait()
 
 
+def hand_out(*refs):
+    given, out, held, sem = refs[:5], refs[5:10], refs[10:14], refs[14]
+    into = [pltpu.make_async_copy(given[i], held[i], sem.at[i]) for i in range(4)]
+    back = [pltpu.make_async_copy(held[i], out[i], sem.at[4 + i]) for i in range(4)]
+    for m in into:
+        m.start()
+    for r in range(DROWS):
+        out[4][r] = given[4][2 * r:2 * r + 2, :].astype(BF)
+    for m, n in zip(into, back):
+        m.wait()
+        n.start()
+    for n in back:
+        n.wait()
+
+
 def on_device(tokens, token_ids, out_grad, w_query, w_key, w_value, dec_states, cache_lens, key_cache, value_cache):
     anywhere = pl.BlockSpec(memory_space=pl.ANY)
     vmem = pl.BlockSpec(memory_space=pltpu.VMEM)
@@ -466,9 +509,9 @@
         return pltpu.VMEM(shape, dtype)
 
     shapes = [(ROWS, QC), (ROWS, HD), (ROWS, HD), (TOK, FEAT), (DEC, QC)]
-    *grads, dec_out = pl.pallas_call(
+    results = pl.pallas_call(
         kernel,
-        out_shape=[jax.ShapeDtypeStruct(s, BF) for s in shapes],
+        out_shape=[jax.ShapeDtypeStruct(s, F32 if s[0] == DEC else BF) for s in shapes],
         in_specs=[vmem, pl.BlockSpec(memory_space=pltpu.SMEM)] + [anywhere] * 8,
         out_specs=[anywhere] * 4 + [vmem],
         scratch_shapes=[
@@ -480,16 +523,25 @@
             buf(8, TOK, FEAT), buf(2, TOK // 2, FEAT), buf(2, TOK // 2, FEAT), buf(2, TOK, FEAT), buf(2, TOK, FEAT),
             buf(TOK, FEAT), buf(TOK, FEAT), buf(ROWS, COLS),
             buf(DROWS, CACHE, HD), buf(DROWS, CACHE, HD),
-            buf(DEC, D), buf(NF * DEC, ROWS), buf(NF * DEC, COLS), buf(NF * DEC, COLS), buf(DEC, QC, dtype=F32),
+            buf(DROWS, 2, D), buf(DEC, D, dtype=F32), buf(DEC, D), buf(NF * DEC, ROWS), buf(NF * DEC, COLS), buf(NF * DEC, COLS),
             pltpu.SemaphoreType.DMA((N_MSG,)), pltpu.SemaphoreType.DMA((N_MSG,)), pltpu.SemaphoreType.DMA((N_LOCAL,)),
         ],
         compiler_params=pltpu.CompilerParams(collective_id=0, has_side_effects=True, vmem_limit_bytes=60 << 20),
         cost_estimate=pl.CostEstimate(flops=13 * 10**9, bytes_accessed=16 * 10**6, transcendentals=2 * 10**6),
     )(
         token_ids.reshape(1, TOK), cache_lens, tokens, out_grad, w_query, w_key, w_value,
-        dec_states.reshape(DEC, D), key_cache, value_cache,
+        dec_states, key_cache, value_cache,
     )
-    return (*grads, dec_out.reshape(DROWS, 2, QC))
+    shapes[4] = (DROWS, 2, QC)
+    return tuple(
+        pl.pallas_call(
+            hand_out,
+            out_shape=[jax.ShapeDtypeStruct(s, BF) for s in shapes],
+            in_specs=[anywhere] * 4 + [vmem],
+            out_specs=[anywhere] * 4 + [vmem],
+            scratch_shapes=[buf(*s) for s in shapes[:4]] + [pltpu.SemaphoreType.DMA((8,))],
+        )(*results)
+    )
 
 
 def solution(mesh):

time: 109 us -> 96.1 us (0.88)
  local copies, waits for them, and re-layouts: 9.43 us -> 0 us
  Pallas kernels: 98.2 us -> 95.3 us
    unnamed x4 -> x0, local copies, waits for them, and re-layouts: 6.48 us -> none
    reshape x2 -> x0, local copies, waits for them, and re-layouts: 2.95 us -> none  [the longest x1 1.61 us: on_device(): dec_states.reshape(DEC, D)]
    pallas_call x1 -> x2, Pallas kernels: 98.2 us -> 95.3 us  [the longest x1 91.9 us: on_device(): pl.pallas_call(kernel, out_shape=[jax.ShapeDtypeStruct(s, F32 if s[0] ==...]
where the time goes in v2:
time: 96.1 us; the launch traced here: 95.9 us
  Pallas kernels  95.3 us (99%)
    pallas_call x1, Pallas kernels, on_device(): pl.pallas_call(kernel, out_shape=[jax.ShapeDtypeStruct(s, F32 if s[0] ==...  91.9 us
    pallas_call x1, Pallas kernels, on_device(): pl.pallas_call(hand_out, out_shape=[jax.ShapeDtypeStruct(s, BF) for s in...  3.41 us

profile of v2, /device:TPU:1, one launch (start us, length us, event | category | flops | bytes accessed | tf_op | source)
XLA Modules:
  0.0 95.9 jit_solution(6000173206995096972)
XLA Ops:
  0.6 91.9 %shard_map.137 = (bf16[256,512]{1,0:T(8,128)(2,1)}, bf16[256,128]{1,0:T(8,128)(2,1)}, bf16[256,128]{1,0:T(8,128)(2,1)}, bf16[512,512]{1,0:T(8,128)(2,1)}, f32[16,512]{1,0:T(8,128)}) custom-call(s32[1,512]{1,0:T(1,128)} %bitcast.1, s32[8]{0:T(128)} %lens.1, bf16[512,4096]{1,0:T(8,128)(2,1)} %tok_h.1, bf16[512,512]{1,0:T(8,128)(2,1)} %og_h.1, ...), custom_call_target="tpu_custom_call" | custom-call | flops 12999999488 | bytes 16000000 | tf_op jit(solution)/shard_map/pallas_call | solution.py:512
  92.5 3.4 %shard_map.138 = (bf16[256,512]{1,0:T(8,128)(2,1)}, bf16[256,128]{1,0:T(8,128)(2,1)}, bf16[256,128]{1,0:T(8,128)(2,1)}, bf16[512,512]{1,0:T(8,128)(2,1)}, bf16[8,2,512]{2,1,0:T(2,128)(2,1)}) custom-call(bf16[256,512]{1,0:T(8,128)(2,1)} %get-tuple-element.10.refs_0_, bf16[256,128]{1,0:T(8,128)(2,1)} %get-tuple-element.11.refs_1_, ...), custom_call_target="tpu_custom_call" | custom-call | tf_op jit(solution)/shard_map/pallas_call | solution.py:537

commit v3 on v2

--- a/solution.py
+++ b/solution.py
@@ -38,10 +38,11 @@
 T_X = 52
 D_IN = 53
 D_OUT = 69
-N_MSG = 85
-
-L_TOK, L_OG, L_WQ, L_WK, L_WV, L_DEC, L_KC, L_VC, L_OWN, L_GQ, L_GK, L_GV, L_IG, L_DO, L_OWN2 = range(15)
-N_LOCAL = 15
+T_X2 = 85
+N_MSG = 86
+
+L_TOK, L_OG, L_WQ, L_WK, L_WV, L_DEC, L_KC, L_VC, L_OWN, L_GQ, L_GK, L_GV, L_IG, L_DO, L_OWN2, L_IDS, L_LENS, L_IG2 = range(18)
+N_LOCAL = 18
 
 NT = (((1,), (1,)), ((), ()))
 
@@ -55,12 +56,12 @@
 
 
 def kernel(
-    ids, lens, tok_h, og_h, wq_h, wk_h, wv_h, dec_h, kc_h, vc_h,
+    ids_h, lens_h, tok_h, og_h, wq_h, wk_h, wv_h, dec_h, kc_h, vc_h,
     gq_o, gk_o, gv_o, ig_o, do_o,
     tok, tok_t, w, proj, pb, og, bias, acts, key_t, gk_acc, gv_acc,
     sbs, acc, rx1, rx0, rm, rp, qm, qp, rfm, rfp,
     part, tfm, tfp, tm, tp, tx, ig, gout,
-    kc, vc, dec3, dec_f32, dec, dec_in, dp, dpr,
+    ids, lens, kc, vc, dec3, dec_f32, dec, dec_in, dp, dpr,
     ssem, rsem, lsem,
 ):
     f = lax.axis_index("fsdp")
@@ -116,6 +117,10 @@
     ]
     for m in loads:
         m.start()
+    load_ids = local(ids_h, ids, L_IDS)
+    load_ids.start()
+    load_lens = local(lens_h, lens, L_LENS)
+    load_lens.start()
     load_tok = local(tok_h, tok, L_TOK)
     load_tok.start()
     load_dec = local(dec_h, dec3, L_DEC)
@@ -140,6 +145,7 @@
     load_kc.start()
     load_vc.start()
 
+    load_ids.wait()
     bos = (ids[...] == BOS_ID).astype(F32)
     row = lax.broadcasted_iota(jnp.int32, (TOK, TOK), 0)
     col = lax.broadcasted_iota(jnp.int32, (TOK, TOK), 1)
@@ -279,7 +285,7 @@
             acts[qs, at] = f32_dot(key_t[:, ks], dscore).T.astype(BF)
         return carry
 
-    lax.fori_loop(0, GROUPS, head, 0)
+    lax.fori_loop(0, GROUPS, head, 0, unroll=True)
     acts[:, QC:QC + HD] = gk_acc[...].astype(BF)
     acts[:, QC + HD:] = gv_acc[...].astype(BF)
 
@@ -293,17 +299,14 @@
     def to_sib(i):
         return msg(R_SIB + i, sbs.at[i], acc.at[i], sib)
 
-    def sib_block(k, carry):
-        i = 7 - k
+    def sib_block(i):
         sbs[i] = grad_block(block_of(i, 1)).astype(BF)
         to_sib(i).start()
-        return carry
-
-    def own_block(i, carry):
+
+    def own_block(i):
         block = grad_block(block_of(i, 0))
         arrived(R_SIB + i, acc.at[i], sib)
         acc[i] = (block + acc[i].astype(F32)).astype(BF)
-        return carry
 
     def sums(dx, dz, part=None):
         ref = acc.at[place_of(dx, dz)]
@@ -317,15 +320,17 @@
 
     t_top, t_bottom = pl.ds(0, TOK // 2), pl.ds(TOK // 2, TOK // 2)
 
-    def input_block(i, carry):
+    def input_block(i):
         rows = w[pl.ds(tid(i // 4, i % 4) * 2, 2)].reshape(2 * ROWS, COLS)
         part[i] = f32_dot_nt(acts[...], rows).astype(BF)
-        return carry
-
-    def send_near(dx):
+
+    def send_far(dx):
         base, i = T_BASE + dx * 6, dx * 4
         send(base + T_PF, part.at[i + 2, t_top], tfp.at[dx], yp)
         send(base + T_MF, part.at[i + 2, t_bottom], tfm.at[dx], ym)
+
+    def send_near(dx):
+        base, i = T_BASE + dx * 6, dx * 4
         send(base + T_PB, part.at[i + 1, t_bottom], tm.at[dx, t_bottom], yp)
         send(base + T_MB, part.at[i + 3, t_top], tp.at[dx, t_top], ym)
 
@@ -345,40 +350,54 @@
         arrived(base + T_PA, tm.at[dx, t_top], yp)
         arrived(base + T_MA, tp.at[dx, t_bottom], ym)
 
-    lax.fori_loop(0, 8, sib_block, 0)
-    lax.fori_loop(4, 8, own_block, 0)
+    input_block(6)
+    send_far(1)
+    input_block(5)
+    input_block(7)
+    send_near(1)
+    for i in (6, 5, 7, 4):
+        sib_block(i)
+    own_block(6)
     send(R_X1T, sums(1, 2, top), rx1.at[top], xp)
     send(R_X1B, sums(1, 2, bottom), rx1.at[bottom], xp)
+    own_block(5)
+    own_block(7)
     send(R_PQ, sums(1, 1), qm, zp)
     send(R_MQ, sums(1, 3), qp, zm)
-    lax.fori_loop(4, 8, input_block, 0)
-    send_near(1)
-    lax.fori_loop(0, 4, own_block, 0)
-    lax.fori_loop(0, 4, input_block, 0)
-
+    own_block(4)
+    for i in (2, 1, 3, 0):
+        sib_block(i)
+    for i in (2, 1, 3):
+        input_block(i)
+
+    send_relayed(1)
+    send_far(0)
+    send_near(0)
+    for i in (2, 1, 3, 0):
+        own_block(i)
     arrived(R_X1T, rx1.at[top], xp)
     add(sums(0, 2, top), rx1.at[top])
     send(R_PF, sums(0, 2, top), rfp, zp)
     send(R_PB, sums(0, 1, bottom), rm.at[bottom], zp)
     send(R_MB, sums(0, 3, top), rp.at[top], zm)
-    send_relayed(1)
-    send_near(0)
     arrived(R_X1B, rx1.at[bottom], xp)
     add(sums(0, 2, bottom), rx1.at[bottom])
     send(R_MF, sums(0, 2, bottom), rfm, zm)
+    input_block(4)
     arrived(R_PQ, qm, zp)
     arrived(R_MQ, qp, zm)
     add(sums(1, 0), qm, qp)
     send(R_X2, sums(1, 0), rx0, xp)
+    input_block(0)
     arrived(R_PF, rfp, zp)
     add(sums(0, 1, top), rfp)
     send(R_PA, sums(0, 1, top), rm.at[top], zp)
+    ring_arrived(1)
+    add(part.at[4], tm.at[1], tp.at[1])
+    send(T_X, part.at[4, t_top], tx.at[t_top], xt)
     arrived(R_MF, rfm, zm)
     add(sums(0, 3, bottom), rfm)
     send(R_MA, sums(0, 3, bottom), rp.at[bottom], zm)
-    ring_arrived(1)
-    add(part.at[4], tm.at[1], tp.at[1])
-    send(T_X, part.at[4], tx, xt)
     send_relayed(0)
 
     arrived(R_PB, rm.at[bottom], zp)
@@ -421,9 +440,21 @@
         return carry
 
     lax.fori_loop(1, NF, send_dec_out, 0)
+    send(T_X2, part.at[4, t_bottom], tx.at[t_bottom], xt)
     own_rows = pl.ds(pl.multiple_of(f * DEC, DEC), DEC)
     own_part = local(dp.at[own_rows, :], dpr.at[own_rows, :], L_OWN2)
     own_part.start()
+    def input_half(rows, i):
+        total = part[0, rows].astype(F32) + tm[0, rows].astype(F32) + tp[0, rows].astype(F32) + tx[rows, :].astype(F32)
+        ig[rows, :] = total.astype(BF)
+        store = local(ig.at[rows], ig_o.at[rows], i)
+        store.start()
+        stores.append(store)
+
+    ring_arrived(0)
+    arrived(T_X, tx.at[t_top], xt)
+    input_half(t_top, L_IG)
+    load_lens.wait()
     load_kc.wait()
     load_vc.wait()
 
@@ -459,14 +490,8 @@
         for g in range(GROUPS):
             do_o[2 * r:2 * r + 2, g * HD:(g + 1) * HD] = mixed[2 * g:2 * g + 2, :]
 
-    ring_arrived(0)
-    arrived(T_X, tx, xt)
-    total = part[0].astype(F32) + tm[0].astype(F32) + tp[0].astype(F32) + tx[...].astype(F32)
-    ig[...] = total.astype(BF)
-    store_ig = local(ig, ig_o, L_IG)
-    store_ig.start()
-    stores.append(store_ig)
-
+    arrived(T_X2, tx.at[t_bottom], xt)
+    input_half(t_bottom, L_IG2)
     for m in sent:
         m.wait_send()
 
@@ -512,7 +537,7 @@
     results = pl.pallas_call(
         kernel,
         out_shape=[jax.ShapeDtypeStruct(s, F32 if s[0] == DEC else BF) for s in shapes],
-        in_specs=[vmem, pl.BlockSpec(memory_space=pltpu.SMEM)] + [anywhere] * 8,
+        in_specs=[anywhere] * 10,
         out_specs=[anywhere] * 4 + [vmem],
         scratch_shapes=[
             buf(TOK, D), buf(D, TOK), buf(NF, ROWS, COLS), buf(TOK, COLS, dtype=F32), buf(TOK, COLS), buf(TOK, QC),
@@ -522,6 +547,7 @@
             buf(HALF, COLS), buf(HALF, COLS),
             buf(8, TOK, FEAT), buf(2, TOK // 2, FEAT), buf(2, TOK // 2, FEAT), buf(2, TOK, FEAT), buf(2, TOK, FEAT),
             buf(TOK, FEAT), buf(TOK, FEAT), buf(ROWS, COLS),
+            buf(1, TOK, dtype=jnp.int32), pltpu.SMEM((DROWS,), jnp.int32),
             buf(DROWS, CACHE, HD), buf(DROWS, CACHE, HD),
             buf(DROWS, 2, D), buf(DEC, D, dtype=F32), buf(DEC, D), buf(NF * DEC, ROWS), buf(NF * DEC, COLS), buf(NF * DEC, COLS),
             pltpu.SemaphoreType.DMA((N_MSG,)), pltpu.SemaphoreType.DMA((N_MSG,)), pltpu.SemaphoreType.DMA((N_LOCAL,)),

time: 96.1 us -> 86.4 us (0.90)
  Pallas kernels: 95.3 us -> 85.3 us
    pallas_call x1, Pallas kernels: 91.9 us -> 81.9 us  [on_device(): pl.pallas_call(kernel, out_shape=[jax.ShapeDtypeStruct(s, F32 if s[0] ==...]
where the time goes in v3:
time: 86.4 us; the launch traced here: 86.2 us
  Pallas kernels  85.3 us (99%)
    pallas_call x1, Pallas kernels, on_device(): pl.pallas_call(kernel, out_shape=[jax.ShapeDtypeStruct(s, F32 if s[0] ==...  81.9 us
    pallas_call x1, Pallas kernels, on_device(): pl.pallas_call(hand_out, out_shape=[jax.ShapeDtypeStruct(s, BF) for s in...  3.41 us

profile of v3, /device:TPU:1, one launch (start us, length us, event | category | flops | bytes accessed | tf_op | source)
XLA Modules:
  0.0 86.2 jit_solution(6396179180904110634)
XLA Ops:
  0.6 81.9 %shard_map.137 = (bf16[256,512]{1,0:T(8,128)(2,1)}, bf16[256,128]{1,0:T(8,128)(2,1)}, bf16[256,128]{1,0:T(8,128)(2,1)}, bf16[512,512]{1,0:T(8,128)(2,1)}, f32[16,512]{1,0:T(8,128)}) custom-call(s32[1,512]{1,0:T(1,128)} %bitcast.1, s32[8]{0:T(128)} %lens_h.1, bf16[512,4096]{1,0:T(8,128)(2,1)} %tok_h.1, bf16[512,512]{1,0:T(8,128)(2,1)} %og_h.1, ...), custom_call_target="tpu_custom_call" | custom-call | flops 12999999488 | bytes 16000000 | tf_op jit(solution)/shard_map/pallas_call | solution.py:537
  82.6 3.4 %shard_map.138 = (bf16[256,512]{1,0:T(8,128)(2,1)}, bf16[256,128]{1,0:T(8,128)(2,1)}, bf16[256,128]{1,0:T(8,128)(2,1)}, bf16[512,512]{1,0:T(8,128)(2,1)}, bf16[8,2,512]{2,1,0:T(2,128)(2,1)}) custom-call(bf16[256,512]{1,0:T(8,128)(2,1)} %get-tuple-element.10.refs_0_, bf16[256,128]{1,0:T(8,128)(2,1)} %get-tuple-element.11.refs_1_, ...), custom_call_target="tpu_custom_call" | custom-call | tf_op jit(solution)/shard_map/pallas_call | solution.py:563

commit v4 on v3

--- a/solution.py
+++ b/solution.py
@@ -61,7 +61,7 @@
     tok, tok_t, w, proj, pb, og, bias, acts, key_t, gk_acc, gv_acc,
     sbs, acc, rx1, rx0, rm, rp, qm, qp, rfm, rfp,
     part, tfm, tfp, tm, tp, tx, ig, gout,
-    ids, lens, kc, vc, dec3, dec_f32, dec, dec_in, dp, dpr,
+    ids, lens, kc, vc, dec3, dec_f32, dec, dec_in, dp, dpr, dout, older,
     ssem, rsem, lsem,
 ):
     f = lax.axis_index("fsdp")
@@ -352,10 +352,7 @@
 
     input_block(6)
     send_far(1)
-    input_block(5)
-    input_block(7)
-    send_near(1)
-    for i in (6, 5, 7, 4):
+    for i in (6, 5, 7):
         sib_block(i)
     own_block(6)
     send(R_X1T, sums(1, 2, top), rx1.at[top], xp)
@@ -364,16 +361,19 @@
     own_block(7)
     send(R_PQ, sums(1, 1), qm, zp)
     send(R_MQ, sums(1, 3), qp, zm)
-    own_block(4)
-    for i in (2, 1, 3, 0):
+    input_block(5)
+    input_block(7)
+    send_near(1)
+    for i in (2, 1, 3, 4, 0):
         sib_block(i)
-    for i in (2, 1, 3):
-        input_block(i)
+    input_block(2)
+    input_block(1)
+    input_block(3)
 
     send_relayed(1)
     send_far(0)
     send_near(0)
-    for i in (2, 1, 3, 0):
+    for i in (2, 1, 3, 4, 0):
         own_block(i)
     arrived(R_X1T, rx1.at[top], xp)
     add(sums(0, 2, top), rx1.at[top])
@@ -475,20 +475,32 @@
     dec_v = dsum[:, QC + HD:]
     n_q = 2 * GROUPS
     place = lax.broadcasted_iota(jnp.int32, (n_q, CACHE), 1)
-    new_col = lax.broadcasted_iota(jnp.int32, (n_q, DEC), 1)
-    new_step = lax.broadcasted_iota(jnp.int32, (n_q, DEC), 0) % 2
+    queries = []
     for r in range(DROWS):
-        q = jnp.concatenate([dec_q[2 * r:2 * r + 2, g * HD:(g + 1) * HD] for g in range(GROUPS)], axis=0).astype(BF)
-        older = jnp.where(place < lens[r], f32_dot_nt(q, kc[r]) * scale, MASKED)
-        visible = (new_col // 2 == r) & (new_col % 2 <= new_step)
-        newer = jnp.where(visible, f32_dot_nt(q, dec_k) * scale, MASKED)
-        best = jnp.maximum(jnp.max(older, 1, keepdims=True), jnp.max(newer, 1, keepdims=True))
-        exp_old = jnp.exp(older - best)
-        exp_new = jnp.exp(newer - best)
-        inv = 1.0 / (jnp.sum(exp_old, 1, keepdims=True) + jnp.sum(exp_new, 1, keepdims=True))
-        mixed = f32_dot((exp_old * inv).astype(BF), vc[r]) + f32_dot((exp_new * inv).astype(BF), dec_v)
+        q = jnp.concatenate([dec_q[2 * r:2 * r + 2, g * HD:(g + 1) * HD] for g in range(GROUPS)], axis=0)
+        queries.append(q)
+        older[r * n_q:(r + 1) * n_q, :] = jnp.where(place < lens[r], f32_dot_nt(q.astype(BF), kc[r]) * scale, MASKED)
+    n_all = DROWS * n_q
+    new_col = lax.broadcasted_iota(jnp.int32, (n_all, DEC), 1)
+    new_row = lax.broadcasted_iota(jnp.int32, (n_all, DEC), 0)
+    visible = (new_col // 2 == new_row // n_q) & (new_col % 2 <= new_row % 2)
+    newer = f32_dot_nt(jnp.concatenate(queries, axis=0).astype(BF), dec_k) * scale
+    newer = jnp.where(visible, newer, MASKED)
+    best = jnp.maximum(jnp.max(older[...], 1, keepdims=True), jnp.max(newer, 1, keepdims=True))
+    exp_old = jnp.exp(older[...] - best)
+    exp_new = jnp.exp(newer - best)
+    inv = 1.0 / (jnp.sum(exp_old, 1, keepdims=True) + jnp.sum(exp_new, 1, keepdims=True))
+    older[...] = exp_old * inv
+    from_new = f32_dot((exp_new * inv).astype(BF), dec_v)
+    for r in range(DROWS):
+        at = slice(r * n_q, (r + 1) * n_q)
+        mixed = f32_dot(older[at, :].astype(BF), vc[r]) + from_new[at, :]
         for g in range(GROUPS):
-            do_o[2 * r:2 * r + 2, g * HD:(g + 1) * HD] = mixed[2 * g:2 * g + 2, :]
+            dout[2 * r:2 * r + 2, g * HD:(g + 1) * HD] = mixed[2 * g:2 * g + 2, :]
+
+    store_do = local(dout, do_o, L_DO)
+    store_do.start()
+    stores.append(store_do)
 
     arrived(T_X2, tx.at[t_bottom], xt)
     input_half(t_bottom, L_IG2)
@@ -512,23 +524,24 @@
 
 
 def hand_out(*refs):
-    given, out, held, sem = refs[:5], refs[5:10], refs[10:14], refs[14]
-    into = [pltpu.make_async_copy(given[i], held[i], sem.at[i]) for i in range(4)]
-    back = [pltpu.make_async_copy(held[i], out[i], sem.at[4 + i]) for i in range(4)]
+    given, out, held, cast, sem = refs[:5], refs[5:10], refs[10:15], refs[15], refs[16]
+    sources = (*held[:4], cast)
+    into = [pltpu.make_async_copy(given[i], held[i], sem.at[i]) for i in range(5)]
+    back = [pltpu.make_async_copy(sources[i], out[i], sem.at[5 + i]) for i in range(5)]
     for m in into:
         m.start()
-    for r in range(DROWS):
-        out[4][r] = given[4][2 * r:2 * r + 2, :].astype(BF)
-    for m, n in zip(into, back):
-        m.wait()
-        n.start()
+    for i in range(5):
+        into[i].wait()
+        if i == 4:
+            for r in range(DROWS):
+                cast[r] = held[4][2 * r:2 * r + 2, :].astype(BF)
+        back[i].start()
     for n in back:
         n.wait()
 
 
 def on_device(tokens, token_ids, out_grad, w_query, w_key, w_value, dec_states, cache_lens, key_cache, value_cache):
     anywhere = pl.BlockSpec(memory_space=pl.ANY)
-    vmem = pl.BlockSpec(memory_space=pltpu.VMEM)
 
     def buf(*shape, dtype=BF):
         return pltpu.VMEM(shape, dtype)
@@ -538,7 +551,7 @@
         kernel,
         out_shape=[jax.ShapeDtypeStruct(s, F32 if s[0] == DEC else BF) for s in shapes],
         in_specs=[anywhere] * 10,
-        out_specs=[anywhere] * 4 + [vmem],
+        out_specs=[anywhere] * 5,
         scratch_shapes=[
             buf(TOK, D), buf(D, TOK), buf(NF, ROWS, COLS), buf(TOK, COLS, dtype=F32), buf(TOK, COLS), buf(TOK, QC),
             buf(TOK, TOK, dtype=F32), buf(TOK, COLS), buf(HD, TOK), buf(TOK, HD, dtype=F32), buf(TOK, HD, dtype=F32),
@@ -549,7 +562,8 @@
             buf(TOK, FEAT), buf(TOK, FEAT), buf(ROWS, COLS),
             buf(1, TOK, dtype=jnp.int32), pltpu.SMEM((DROWS,), jnp.int32),
             buf(DROWS, CACHE, HD), buf(DROWS, CACHE, HD),
-            buf(DROWS, 2, D), buf(DEC, D, dtype=F32), buf(DEC, D), buf(NF * DEC, ROWS), buf(NF * DEC, COLS), buf(NF * DEC, COLS),
+            buf(DROWS, 2, D), buf(DEC, D, dtype=F32), buf(DEC, D), buf(NF * DEC, ROWS), buf(NF * DEC, COLS), buf(NF * DEC, COLS), buf(DEC, QC, dtype=F32),
+            buf(DROWS * 2 * GROUPS, CACHE, dtype=F32),
             pltpu.SemaphoreType.DMA((N_MSG,)), pltpu.SemaphoreType.DMA((N_MSG,)), pltpu.SemaphoreType.DMA((N_LOCAL,)),
         ],
         compiler_params=pltpu.CompilerParams(collective_id=0, has_side_effects=True, vmem_limit_bytes=60 << 20),
@@ -563,9 +577,11 @@
         pl.pallas_call(
             hand_out,
             out_shape=[jax.ShapeDtypeStruct(s, BF) for s in shapes],
-            in_specs=[anywhere] * 4 + [vmem],
-            out_specs=[anywhere] * 4 + [vmem],
-            scratch_shapes=[buf(*s) for s in shapes[:4]] + [pltpu.SemaphoreType.DMA((8,))],
+            in_specs=[anywhere] * 5,
+            out_specs=[anywhere] * 5,
+            scratch_shapes=[
+                *[buf(*s) for s in shapes[:4]], buf(DEC, QC, dtype=F32), buf(*shapes[4]), pltpu.SemaphoreType.DMA((10,)),
+            ],
         )(*results)
     )
 

time: 86.4 us -> 83 us (0.961)
  Pallas kernels: 85.3 us -> 81.7 us
    pallas_call x1, Pallas kernels: 81.9 us -> 79.7 us  [on_device(): pl.pallas_call(kernel, out_shape=[jax.ShapeDtypeStruct(s, F32 if s[0] ==...]
    pallas_call x1, Pallas kernels: 3.41 us -> 2.07 us  [on_device(): pl.pallas_call(hand_out, out_shape=[jax.ShapeDtypeStruct(s, BF) for s in...]
where the time goes in v4:
time: 83 us; the launch traced here: 82.6 us
  Pallas kernels  81.7 us (98%)
    pallas_call x1, Pallas kernels, on_device(): pl.pallas_call(kernel, out_shape=[jax.ShapeDtypeStruct(s, F32 if s[0] ==...  79.7 us
    pallas_call x1, Pallas kernels, on_device(): pl.pallas_call(hand_out, out_shape=[jax.ShapeDtypeStruct(s, BF) for s in...  2.07 us

profile of v4, /device:TPU:1, one launch (start us, length us, event | category | flops | bytes accessed | tf_op | source)
XLA Modules:
  0.0 82.6 jit_solution(3077706525021484339)
XLA Ops:
  0.6 79.7 %shard_map.137 = (bf16[256,512]{1,0:T(8,128)(2,1)}, bf16[256,128]{1,0:T(8,128)(2,1)}, bf16[256,128]{1,0:T(8,128)(2,1)}, bf16[512,512]{1,0:T(8,128)(2,1)}, f32[16,512]{1,0:T(8,128)}) custom-call(s32[1,512]{1,0:T(1,128)} %bitcast.1, s32[8]{0:T(128)} %lens_h.1, bf16[512,4096]{1,0:T(8,128)(2,1)} %tok_h.1, bf16[512,512]{1,0:T(8,128)(2,1)} %og_h.1, ...), custom_call_target="tpu_custom_call" | custom-call | flops 12999999488 | bytes 16000000 | tf_op jit(solution)/shard_map/pallas_call | solution.py:550
  80.3 2.1 %shard_map.138 = (bf16[256,512]{1,0:T(8,128)(2,1)}, bf16[256,128]{1,0:T(8,128)(2,1)}, bf16[256,128]{1,0:T(8,128)(2,1)}, bf16[512,512]{1,0:T(8,128)(2,1)}, bf16[8,2,512]{2,1,0:T(2,128)(2,1)}) custom-call(bf16[256,512]{1,0:T(8,128)(2,1)} %get-tuple-element.10.refs_0_, bf16[256,128]{1,0:T(8,128)(2,1)} %get-tuple-element.11.refs_1_, ...), custom_call_target="tpu_custom_call" | custom-call | tf_op jit(solution)/shard_map/pallas_call | solution.py:577

commit v5 on v4

--- a/solution.py
+++ b/solution.py
@@ -39,10 +39,11 @@
 D_IN = 53
 D_OUT = 69
 T_X2 = 85
-N_MSG = 86
-
-L_TOK, L_OG, L_WQ, L_WK, L_WV, L_DEC, L_KC, L_VC, L_OWN, L_GQ, L_GK, L_GV, L_IG, L_DO, L_OWN2, L_IDS, L_LENS, L_IG2 = range(18)
-N_LOCAL = 18
+T_X3 = 86
+N_MSG = 87
+
+L_TOK, L_OG, L_WQ, L_WK, L_WV, L_DEC, L_KC, L_VC, L_OWN, L_GQ, L_GK, L_GV, L_IG, L_DO, L_OWN2, L_IDS, L_LENS, L_IG2, L_IG3 = range(19)
+N_LOCAL = 19
 
 NT = (((1,), (1,)), ((), ()))
 
@@ -319,6 +320,7 @@
         dst[...] = total.astype(BF)
 
     t_top, t_bottom = pl.ds(0, TOK // 2), pl.ds(TOK // 2, TOK // 2)
+    t_third, t_last = pl.ds(TOK // 2, TOK // 4), pl.ds(3 * TOK // 4, TOK // 4)
 
     def input_block(i):
         rows = w[pl.ds(tid(i // 4, i % 4) * 2, 2)].reshape(2 * ROWS, COLS)
@@ -440,7 +442,8 @@
         return carry
 
     lax.fori_loop(1, NF, send_dec_out, 0)
-    send(T_X2, part.at[4, t_bottom], tx.at[t_bottom], xt)
+    send(T_X2, part.at[4, t_third], tx.at[t_third], xt)
+    send(T_X3, part.at[4, t_last], tx.at[t_last], xt)
     own_rows = pl.ds(pl.multiple_of(f * DEC, DEC), DEC)
     own_part = local(dp.at[own_rows, :], dpr.at[own_rows, :], L_OWN2)
     own_part.start()
@@ -502,8 +505,10 @@
     store_do.start()
     stores.append(store_do)
 
-    arrived(T_X2, tx.at[t_bottom], xt)
-    input_half(t_bottom, L_IG2)
+    arrived(T_X2, tx.at[t_third], xt)
+    input_half(t_third, L_IG2)
+    arrived(T_X3, tx.at[t_last], xt)
+    input_half(t_last, L_IG3)
     for m in sent:
         m.wait_send()
 

time: 83 us -> 82.9 us (level)
  no operation moved by 1% of the time
where the time goes in v5:
time: 82.9 us; the launch traced here: 82.5 us
  Pallas kernels  81.7 us (99%)
    pallas_call x1, Pallas kernels, on_device(): pl.pallas_call(kernel, out_shape=[jax.ShapeDtypeStruct(s, F32 if s[0] ==...  79.6 us
    pallas_call x1, Pallas kernels, on_device(): pl.pallas_call(hand_out, out_shape=[jax.ShapeDtypeStruct(s, BF) for s in...  2.07 us

profile of v5, /device:TPU:1, one launch (start us, length us, event | category | flops | bytes accessed | tf_op | source)
XLA Modules:
  0.0 82.5 jit_solution(13772949174477943129)
XLA Ops:
  0.6 79.6 %shard_map.137 = (bf16[256,512]{1,0:T(8,128)(2,1)}, bf16[256,128]{1,0:T(8,128)(2,1)}, bf16[256,128]{1,0:T(8,128)(2,1)}, bf16[512,512]{1,0:T(8,128)(2,1)}, f32[16,512]{1,0:T(8,128)}) custom-call(s32[1,512]{1,0:T(1,128)} %bitcast.1, s32[8]{0:T(128)} %lens_h.1, bf16[512,4096]{1,0:T(8,128)(2,1)} %tok_h.1, bf16[512,512]{1,0:T(8,128)(2,1)} %og_h.1, ...), custom_call_target="tpu_custom_call" | custom-call | flops 12999999488 | bytes 16000000 | tf_op jit(solution)/shard_map/pallas_call | solution.py:555
  80.2 2.1 %shard_map.138 = (bf16[256,512]{1,0:T(8,128)(2,1)}, bf16[256,128]{1,0:T(8,128)(2,1)}, bf16[256,128]{1,0:T(8,128)(2,1)}, bf16[512,512]{1,0:T(8,128)(2,1)}, bf16[8,2,512]{2,1,0:T(2,128)(2,1)}) custom-call(bf16[256,512]{1,0:T(8,128)(2,1)} %get-tuple-element.10.refs_0_, bf16[256,128]{1,0:T(8,128)(2,1)} %get-tuple-element.11.refs_1_, ...), custom_call_target="tpu_custom_call" | custom-call | tf_op jit(solution)/shard_map/pallas_call | solution.py:582
